TPU v7x, 32 devices: a whole 2x2x4 slice. The times are simulated.
32 devices in a mesh: section: 4 (over x, core), seq: 8 (over z, y).
Axes of the slice: x: 2, y: 2, z: 4, core: 2. Of those that a mesh axis runs over, the one named last changes fastest.
Arguments:
- incoming: bfloat16 [4, 8, 16, 24, 320], P(None, 'seq'), may hold values from -6 to 6
- plan: int32 [4], replicated, may hold values from 0 to 3, each once
- waiting: bfloat16 [4, 8, 16, 24, 320], P('section', 'seq'), may hold values from -6 to 6
- spatial_weight: bfloat16 [4, 2, 9, 320, 320], P('section'), may hold values from -0.109375 to 0.109375
- temporal_weight: bfloat16 [4, 2, 3, 320, 320], P('section'), may hold values from -0.1875 to 0.1875
- attn_in: bfloat16 [4, 320, 960], P('section'), may hold values from -5 to 5
- attn_out: bfloat16 [4, 320, 320], P('section'), may hold values from -0.3125 to 0.3125
Outputs:
- outputs: bfloat16 [3, 4, 8, 16, 24, 320], P(None, 'section', 'seq')
Inputs may be any that keep to these rules, and one draw needn't show every extreme that they name: `plan`: each of the 4 clip numbers appears once.
All inputs are finite; a program needn't handle non-finite values.
Results may differ from a plain program's by a relative error of at most 0.02.
Values may be sent and summed in bfloat16 or wider, within the bound.
No kernel may reach another device: no remote copies, remote signals or barrier semaphores. Data moves between devices by JAX's collectives and lax.ppermute only.
A program may use at most 64 MiB of HBM per device.

v0:
```python
import functools

import jax
import jax.numpy as jnp
from jax import lax
from jax.experimental import pallas as pl
from jax.experimental.pallas import tpu as pltpu
from jax.sharding import PartitionSpec as P

HEADS = 5
GROUPS = 32
TICKS = 3
EPSILON = 1e-05
MIB = 1 << 20


def silu(values):
    half = 0.5 * values
    return half + half * jnp.tanh(half)


def bucket(shape, dim, size):
    index = lax.broadcasted_iota(jnp.int32, shape, dim).astype(jnp.float32)
    return jnp.floor((index + 0.5) * (1.0 / size))


def within(shape, dim, size):
    index = lax.broadcasted_iota(jnp.int32, shape, dim).astype(jnp.float32)
    return index - size * jnp.floor((index + 0.5) * (1.0 / size))


def group_total(partial, same_group):
    high = partial.astype(jnp.bfloat16).astype(jnp.float32)
    rest = partial - high
    middle = rest.astype(jnp.bfloat16).astype(jnp.float32)
    low = rest - middle
    rows = jnp.concatenate([high, middle, low, jnp.zeros_like(low)], axis=0).astype(jnp.bfloat16)
    sums = jnp.dot(rows, same_group, preferred_element_type=jnp.float32)
    return jnp.sum(sums, axis=0, keepdims=True)


def group_norm(values, same_group):
    cells, channels = values.shape
    scale = 1.0 / (cells * (channels // GROUPS))
    center = group_total(jnp.sum(values.reshape(-1, 8, channels), axis=0), same_group) * scale
    shifted = values - center
    spread = group_total(jnp.sum(jnp.square(shifted).reshape(-1, 8, channels), axis=0), same_group) * scale
    return shifted * lax.rsqrt(spread + EPSILON)


def layer_norm(values):
    center = jnp.mean(values, axis=-1, keepdims=True)
    shifted = values - center
    spread = jnp.mean(jnp.square(shifted), axis=-1, keepdims=True)
    return shifted * lax.rsqrt(spread + EPSILON)


def spatial_kernel(height, width, picks, *refs):
    if picks:
        pick_ref, entering_ref, passed_ref, weight_ref, out_ref, kernels, taps, sems = refs
    else:
        passed_ref, weight_ref, out_ref, kernels, taps, sems = refs
    cells, channels = out_ref.shape
    copies = []
    for layer in range(2):
        for row in range(3):
            copy = pltpu.make_async_copy(
                weight_ref.at[layer, row], kernels.at[layer, row], sems.at[layer, row]
            )
            copy.start()
            copies.append(copy)
    edge = jnp.zeros((width, 3 * channels), jnp.bfloat16)
    taps[0:width, :] = edge
    taps[width + cells : 2 * width + cells, :] = edge
    same_group = (
        bucket((channels, channels), 0, channels // GROUPS)
        == bucket((channels, channels), 1, channels // GROUPS)
    ).astype(jnp.float32).astype(jnp.bfloat16)
    column = lax.broadcasted_iota(jnp.int32, (1, width, channels), 1)

    def conv(values, layer):
        framed = values.reshape(height, width, channels)
        left = jnp.where(column == 0, 0.0, pltpu.roll(framed, 1, 1)).reshape(cells, channels)
        right = jnp.where(column == width - 1, 0.0, pltpu.roll(framed, width - 1, 1)).reshape(cells, channels)
        taps[width : width + cells, 0:channels] = left.astype(jnp.bfloat16)
        taps[width : width + cells, channels : 2 * channels] = values.astype(jnp.bfloat16)
        taps[width : width + cells, 2 * channels : 3 * channels] = right.astype(jnp.bfloat16)
        total = None
        for row in range(3):
            copies[3 * layer + row].wait()
            part = jnp.dot(
                taps[row * width : row * width + cells, :],
                kernels[layer, row],
                preferred_element_type=jnp.float32,
            )
            total = part if total is None else total + part
        return total

    start = passed_ref[...]
    if picks:
        start = jnp.where(pick_ref[0] == 1, entering_ref[...], start)
    start = start.astype(jnp.float32)
    middle = conv(silu(group_norm(start, same_group)), 0).astype(jnp.bfloat16).astype(jnp.float32)
    after = conv(silu(group_norm(middle, same_group)), 1)
    out_ref[...] = (start + after).astype(jnp.bfloat16)


def spatial_part(height, width, passed, weights, picked=None, entering=None):
    cells, channels = passed.shape
    weights = weights.reshape(2, 3, 3 * channels, weights.shape[-1])
    specs = [
        pl.BlockSpec((cells, channels), lambda i, *_: (0, 0)),
        pl.BlockSpec(memory_space=pl.ANY),
    ]
    operands = [passed, weights]
    if picked is not None:
        specs = [pl.BlockSpec((None, cells, channels), lambda i, pick: (pick[1], 0, 0))] + specs
        operands = [picked, entering] + operands
    return pl.pallas_call(
        functools.partial(spatial_kernel, height, width, picked is not None),
        out_shape=jax.ShapeDtypeStruct((cells, channels), jnp.bfloat16),
        grid_spec=pltpu.PrefetchScalarGridSpec(
            num_scalar_prefetch=0 if picked is None else 1,
            grid=(1,),
            in_specs=specs,
            out_specs=pl.BlockSpec((cells, channels), lambda i, *_: (0, 0)),
            scratch_shapes=[
                pltpu.VMEM(weights.shape, jnp.bfloat16),
                pltpu.VMEM((cells + 2 * width, 3 * channels), jnp.bfloat16),
                pltpu.SemaphoreType.DMA((2, 3)),
            ],
        ),
        compiler_params=pltpu.CompilerParams(vmem_limit_bytes=24 * MIB),
    )(*operands)


def temporal_kernel(frames, items, in_ref, conv_ref, packed_ref, outward_ref, out_ref, kernels, packed, outward, taps, sems):
    rows, channels = out_ref.shape
    copies = [
        pltpu.make_async_copy(conv_ref.at[0], kernels.at[0], sems.at[0]),
        pltpu.make_async_copy(conv_ref.at[1], kernels.at[1], sems.at[1]),
        pltpu.make_async_copy(packed_ref, packed, sems.at[2]),
        pltpu.make_async_copy(outward_ref, outward, sems.at[3]),
    ]
    for copy in copies:
        copy.start()
    aligned = items % 16 == 0

    def conv(values, layer):
        if aligned:
            whole = values.astype(jnp.bfloat16)
            edge = jnp.zeros((items, channels), jnp.bfloat16)
            taps[0:items, 0:channels] = edge
            taps[items:rows, 0:channels] = whole[0 : rows - items]
            taps[:, channels : 2 * channels] = whole
            taps[0 : rows - items, 2 * channels : 3 * channels] = whole[items:rows]
            taps[rows - items : rows, 2 * channels : 3 * channels] = edge
        else:
            row = lax.broadcasted_iota(jnp.int32, (rows, channels), 0)
            before = jnp.where(row < items, 0.0, pltpu.roll(values, items, 0))
            behind = jnp.where(row >= rows - items, 0.0, pltpu.roll(values, rows - items, 0))
            taps[:, 0:channels] = before.astype(jnp.bfloat16)
            taps[:, channels : 2 * channels] = values.astype(jnp.bfloat16)
            taps[:, 2 * channels : 3 * channels] = behind.astype(jnp.bfloat16)
        copies[layer].wait()
        return jnp.dot(taps[...], kernels[layer], preferred_element_type=jnp.float32)

    start = in_ref[...].astype(jnp.float32)
    middle = conv(silu(layer_norm(start)), 0).astype(jnp.bfloat16).astype(jnp.float32)
    after = (start + conv(silu(layer_norm(middle)), 1)).astype(jnp.bfloat16).astype(jnp.float32)

    normed = layer_norm(after).astype(jnp.bfloat16)
    copies[2].wait()
    taps[...] = jnp.dot(normed, packed[...], preferred_element_type=jnp.float32).astype(jnp.bfloat16)
    queries = taps[:, 0:channels]
    keys = taps[:, channels : 2 * channels]
    values = taps[:, 2 * channels : 3 * channels]

    head_size = channels // HEADS
    block = 16 if aligned else items
    size = frames * block
    apart = within((size, size), 0, block) != within((size, size), 1, block)
    blocked = jnp.where(apart, -1e30, 0.0)
    copies[3].wait()
    mixed_blocks = []
    for first in range(0, items, block):
        def part(whole):
            if block == items:
                return whole
            return jnp.concatenate(
                [whole[f * items + first : f * items + first + block] for f in range(frames)], axis=0
            )

        q, k, v = part(queries), part(keys), part(values)
        mixed = []
        for head in range(HEADS):
            lanes = slice(head * head_size, (head + 1) * head_size)
            scores = lax.dot_general(
                q[:, lanes], k[:, lanes], (((1,), (1,)), ((), ())), preferred_element_type=jnp.float32
            ) * head_size ** (-0.5) + blocked
            top = jnp.max(scores, axis=-1, keepdims=True)
            raised = jnp.exp(scores - top)
            weights = (raised / jnp.sum(raised, axis=-1, keepdims=True)).astype(jnp.bfloat16)
            mixed.append(jnp.dot(weights, v[:, lanes], preferred_element_type=jnp.float32))
        mixed_blocks.append(jnp.concatenate(mixed, axis=1).astype(jnp.bfloat16))
    if len(mixed_blocks) == 1:
        mixed = mixed_blocks[0]
    else:
        mixed = jnp.concatenate(
            [piece[f * block : (f + 1) * block] for f in range(frames) for piece in mixed_blocks], axis=0
        )
    result = after + jnp.dot(mixed, outward[...], preferred_element_type=jnp.float32)
    out_ref[...] = result.astype(jnp.bfloat16)


def temporal_part(frames, items, values, kernels, packed, outward):
    rows, channels = values.shape
    kernels = kernels.reshape(2, 3 * channels, kernels.shape[-1])
    anywhere = pl.BlockSpec(memory_space=pl.ANY)
    return pl.pallas_call(
        functools.partial(temporal_kernel, frames, items),
        out_shape=jax.ShapeDtypeStruct((rows, channels), jnp.bfloat16),
        in_specs=[pl.BlockSpec(memory_space=pltpu.VMEM), anywhere, anywhere, anywhere],
        out_specs=pl.BlockSpec(memory_space=pltpu.VMEM),
        scratch_shapes=[
            pltpu.VMEM(kernels.shape, jnp.bfloat16),
            pltpu.VMEM(packed.shape, jnp.bfloat16),
            pltpu.VMEM(outward.shape, jnp.bfloat16),
            pltpu.VMEM((rows, 3 * channels), jnp.bfloat16),
            pltpu.SemaphoreType.DMA((4,)),
        ],
        compiler_params=pltpu.CompilerParams(vmem_limit_bytes=24 * MIB),
    )(values, kernels, packed, outward)


def shards(incoming, plan, waiting, spatial_weight, temporal_weight, attn_in, attn_out):
    clips, _, height, width, channels = incoming.shape
    cells = height * width
    devices = lax.axis_size("seq")
    share = cells // devices
    sections = lax.axis_size("section")
    first_section = (lax.axis_index("section") == 0).astype(jnp.int32)
    entering = incoming.reshape(clips, cells, channels)
    current = waiting.reshape(cells, channels)
    collected = []
    for tick in range(TICKS):
        if tick == 0:
            after = spatial_part(height, width, current, spatial_weight[0])
        else:
            ring = [(i, (i + 1) % sections) for i in range(sections)]
            passed = lax.ppermute(current, "section", ring)
            picked = jnp.stack([first_section, plan[tick - 1]])
            after = spatial_part(height, width, passed, spatial_weight[0], picked, entering)
        grouped = after.reshape(devices, share, channels)
        gathered = lax.all_to_all(grouped, "seq", split_axis=0, concat_axis=0, tiled=True)
        done = temporal_part(
            devices, share, gathered.reshape(devices * share, channels), temporal_weight[0], attn_in[0], attn_out[0]
        )
        back = lax.all_to_all(
            done.reshape(devices, share, channels), "seq", split_axis=0, concat_axis=0, tiled=True
        )
        current = back.reshape(cells, channels)
        collected.append(current.reshape(height, width, channels))
    return jnp.stack(collected)[:, None, None]


def solution(mesh):
    return jax.shard_map(
        shards,
        mesh=mesh,
        in_specs=(
            P(None, "seq", None, None, None),
            P(),
            P("section", "seq", None, None, None),
            P("section", None, None, None, None),
            P("section", None, None, None, None),
            P("section", None, None),
            P("section", None, None),
        ),
        out_specs=P(None, "section", "seq", None, None, None),
        check_vma=False,
    )
```

profile of v0, /device:TPU:0, one launch (start us, length us, event | category | flops | bytes accessed | tf_op | source)
XLA Modules:
  0.0 147.6 jit_solution(9800429129291408668)
XLA Ops:
  0.0 2.3 %copy-done = bf16[1,2,9,320,320]{4,3,2,1,0:T(8,128)(2,1)S(1)} copy-done((bf16[1,2,9,320,320]{4,3,2,1,0:T(8,128)(2,1)S(1)}, bf16[1,2,9,320,320]{4,3,2,1,0:T(8,128)(2,1)}, u32[]{:S(2)}) %copy-start) | copy-done | bytes 3686424
  2.3 1.0 copy-done.7
  3.2 6.8 %shard_map.73 = bf16[384,320]{1,0:T(8,128)(2,1)S(1)} custom-call(bf16[384,320]{1,0:T(8,128)(2,1)S(1)} %bitcast.48, bf16[2,3,960,320]{3,2,1,0:T(8,128)(2,1)S(1)} %bitcast.23), custom_call_target="tpu_custom_call" | custom-call | tf_op jit(solution)/shard_map/pallas_call | solution.py:119
  10.0 17.4 %all_to_all.30 = bf16[8,48,320]{2,1,0:T(8,128)(2,1)S(1)} all-to-all(bf16[8,48,320]{2,1,0:T(8,128)(2,1)S(1)} %bitcast.47), channel_id=1, replica_groups=mesh['section'=4,'seq'=8] {'seq'}, dimensions={0} | all-to-all | bytes 491520 | tf_op jit(solution)/shard_map/all_to_all | solution.py:255
  27.4 0.0 copy-done.2
  27.4 0.0 copy-done.3
  27.4 0.0 copy-done.5
  27.4 0.0 copy-start.8
  27.4 0.0 copy-start.4
  27.5 8.9 %shard_map.74 = bf16[384,320]{1,0:T(8,128)(2,1)S(1)} custom-call(bf16[384,320]{1,0:T(8,128)(2,1)S(1)} %bitcast.41, bf16[2,960,320]{2,1,0:T(8,128)(2,1)S(1)} %bitcast.28, bf16[320,960]{1,0:T(8,128)(2,1)S(1)} %bitcast.31, bf16[320,320]{1,0:T(8,128)(2,1)S(1)} %bitcast.36), custom_call_target="tpu_custom_call" | custom-call | tf_op jit(solution)/shard_map/pallas_call | solution.py:220
  36.4 0.0 slice-start
  36.4 13.1 %all_to_all.31 = bf16[8,48,320]{2,1,0:T(8,128)(2,1)} all-to-all(bf16[8,48,320]{2,1,0:T(8,128)(2,1)S(1)} %bitcast.42), channel_id=1, replica_groups=mesh['section'=4,'seq'=8] {'seq'}, dimensions={0} | all-to-all | bytes 491520 | tf_op jit(solution)/shard_map/all_to_all | solution.py:259
  49.5 0.0 collective-permute-start
  49.5 0.0 copy-done.8
  49.5 0.6 fusion
  50.1 0.7 pad_add_fusion.refs_0_
  50.8 5.1 %collective-permute-done.refs_2_ = bf16[384,320]{1,0:T(8,128)(2,1)} collective-permute-done((bf16[384,320]{1,0:T(8,128)(2,1)}, bf16[384,320]{1,0:T(8,128)(2,1)}, u32[]{:S(2)}, u32[]{:S(2)}) %collective-permute-start) | collective-permute-done | bytes 245792 | tf_op jit(solution)/shard_map/ppermute | solution.py:251
  55.9 0.0 copy-done.4
  55.9 2.3 %copy-done.1 = bf16[1,2,9,320,320]{4,3,2,1,0:T(8,128)(2,1)S(1)} copy-done((bf16[1,2,9,320,320]{4,3,2,1,0:T(8,128)(2,1)S(1)}, bf16[1,2,9,320,320]{4,3,2,1,0:T(8,128)(2,1)}, u32[]{:S(2)}) %copy-start.1) | copy-done | bytes 3686424
  58.2 8.5 %shard_map.75 = bf16[384,320]{1,0:T(8,128)(2,1)S(1)} custom-call(s32[2]{0:T(128)S(1)} %pad_add_fusion.refs_0_, bf16[4,384,320]{2,1,0:T(8,128)(2,1)S(1)} %bitcast.34, bf16[384,320]{1,0:T(8,128)(2,1)} %collective-permute-done.refs_2_, bf16[2,3,960,320]{3,2,1,0:T(8,128)(2,1)S(1)} %bitcast.24), custom_call_target="tpu_custom_call" | custom-call | tf_op jit(solution)/shard_map/pallas_call | solution.py:119
  66.7 12.3 %all_to_all.32 = bf16[8,48,320]{2,1,0:T(8,128)(2,1)S(1)} all-to-all(bf16[8,48,320]{2,1,0:T(8,128)(2,1)S(1)} %bitcast.39), channel_id=1, replica_groups=mesh['section'=4,'seq'=8] {'seq'}, dimensions={0} | all-to-all | bytes 491520 | tf_op jit(solution)/shard_map/all_to_all | solution.py:255
  79.0 8.9 %shard_map.76 = bf16[384,320]{1,0:T(8,128)(2,1)S(1)} custom-call(bf16[384,320]{1,0:T(8,128)(2,1)S(1)} %bitcast.43, bf16[2,960,320]{2,1,0:T(8,128)(2,1)S(1)} %bitcast.29, bf16[320,960]{1,0:T(8,128)(2,1)S(1)} %bitcast.32, bf16[320,320]{1,0:T(8,128)(2,1)S(1)} %bitcast.37), custom_call_target="tpu_custom_call" | custom-call | tf_op jit(solution)/shard_map/pallas_call | solution.py:220
  87.9 12.5 %all_to_all.33 = bf16[8,48,320]{2,1,0:T(8,128)(2,1)S(1)} all-to-all(bf16[8,48,320]{2,1,0:T(8,128)(2,1)S(1)} %bitcast.44), channel_id=1, replica_groups=mesh['section'=4,'seq'=8] {'seq'}, dimensions={0} | all-to-all | bytes 491520 | tf_op jit(solution)/shard_map/all_to_all | solution.py:259
  100.4 0.0 collective-permute-start.1
  100.4 0.7 pad_add_fusion.1.refs_0_
  101.1 5.4 %collective-permute-done.1.refs_2_ = bf16[384,320]{1,0:T(8,128)(2,1)S(1)} collective-permute-done((bf16[384,320]{1,0:T(8,128)(2,1)S(1)}, bf16[384,320]{1,0:T(8,128)(2,1)S(1)}, u32[]{:S(2)}, u32[]{:S(2)}) %collective-permute-start.1) | collective-permute-done | bytes 245792 | tf_op jit(solution)/shard_map/ppermute | solution.py:251
  106.6 0.0 slice-done
  106.6 7.3 %shard_map.77 = bf16[384,320]{1,0:T(8,128)(2,1)S(1)} custom-call(s32[2]{0:T(128)S(1)} %pad_add_fusion.1.refs_0_, bf16[4,384,320]{2,1,0:T(8,128)(2,1)S(1)} %bitcast.35, bf16[384,320]{1,0:T(8,128)(2,1)S(1)} %collective-permute-done.1.refs_2_, bf16[2,3,960,320]{3,2,1,0:T(8,128)(2,1)S(1)} %bitcast.27), custom_call_target="tpu_custom_call" | custom-call | tf_op jit(solution)/shard_map/pallas_call | solution.py:119
  113.9 11.4 %all_to_all.34 = bf16[8,48,320]{2,1,0:T(8,128)(2,1)S(1)} all-to-all(bf16[8,48,320]{2,1,0:T(8,128)(2,1)S(1)} %bitcast.40), channel_id=1, replica_groups=mesh['section'=4,'seq'=8] {'seq'}, dimensions={0} | all-to-all | bytes 491520 | tf_op jit(solution)/shard_map/all_to_all | solution.py:255
  125.4 8.9 %shard_map.78 = bf16[384,320]{1,0:T(8,128)(2,1)S(1)} custom-call(bf16[384,320]{1,0:T(8,128)(2,1)S(1)} %bitcast.45, bf16[2,960,320]{2,1,0:T(8,128)(2,1)S(1)} %bitcast.30, bf16[320,960]{1,0:T(8,128)(2,1)S(1)} %bitcast.33, bf16[320,320]{1,0:T(8,128)(2,1)S(1)} %bitcast.38), custom_call_target="tpu_custom_call" | custom-call | tf_op jit(solution)/shard_map/pallas_call | solution.py:220
  134.3 11.3 %all_to_all.35 = bf16[8,48,320]{2,1,0:T(8,128)(2,1)S(1)} all-to-all(bf16[8,48,320]{2,1,0:T(8,128)(2,1)S(1)} %bitcast.46), channel_id=1, replica_groups=mesh['section'=4,'seq'=8] {'seq'}, dimensions={0} | all-to-all | bytes 491520 | tf_op jit(solution)/shard_map/all_to_all | solution.py:259
  145.5 2.1 %maximum_bitcast_fusion = bf16[3,1,1,16,24,320]{5,4,3,2,1,0:T(8,128)(2,1)} fusion(bf16[1,16,24,320]{3,2,1,0:T(8,128)(2,1)S(1)} %bitcast.51, bf16[1,16,24,320]{3,2,1,0:T(8,128)(2,1)S(1)} %bitcast.50, bf16[1,16,24,320]{3,2,1,0:T(8,128)(2,1)} %bitcast.8), kind=kLoop, calls=%fused_computation | loop fusion | flops 737280 | bytes 1474560 | tf_op jit(solution)/shard_map/broadcast_in_dim | solution.py:264
  (11 shorter events, 0.0 us)
Async XLA Ops:
  0.0 2.3 %copy-start = (bf16[1,2,9,320,320]{4,3,2,1,0:T(8,128)(2,1)S(1)}, bf16[1,2,9,320,320]{4,3,2,1,0:T(8,128)(2,1)}, u32[]{:S(2)}) copy-start(bf16[1,2,9,320,320]{4,3,2,1,0:T(8,128)(2,1)} %param.10) | copy-start | bytes 11059204
  2.3 1.0 copy-start.7
  3.2 24.2 %copy-start.2 = (bf16[1,2,3,320,320]{4,3,2,1,0:T(8,128)(2,1)S(1)}, bf16[1,2,3,320,320]{4,3,2,1,0:T(8,128)(2,1)}, u32[]{:S(2)}) copy-start(bf16[1,2,3,320,320]{4,3,2,1,0:T(8,128)(2,1)} %param.11) | copy-start | bytes 3686404
  3.2 24.2 %copy-start.3 = (bf16[1,320,960]{2,1,0:T(8,128)(2,1)S(1)}, bf16[1,320,960]{2,1,0:T(8,128)(2,1)}, u32[]{:S(2)}) copy-start(bf16[1,320,960]{2,1,0:T(8,128)(2,1)} %param.12) | copy-start | bytes 1843204
  3.2 24.2 %copy-start.5 = (bf16[1,320,320]{2,1,0:T(8,128)(2,1)S(1)}, bf16[1,320,320]{2,1,0:T(8,128)(2,1)}, u32[]{:S(2)}) copy-start(bf16[1,320,320]{2,1,0:T(8,128)(2,1)} %param.13) | copy-start | bytes 614404
  27.4 22.0 %copy-start.8 = (s32[4]{0:T(128)S(1)}, s32[4]{0:T(128)}, u32[]{:S(2)}) copy-start(s32[4]{0:T(128)} %param.8) | copy-start | bytes 52
  27.4 28.5 %copy-start.4 = (bf16[4,1,16,24,320]{4,3,2,1,0:T(8,128)(2,1)S(1)}, bf16[4,1,16,24,320]{4,3,2,1,0:T(8,128)(2,1)}, u32[]{:S(2)}) copy-start(bf16[4,1,16,24,320]{4,3,2,1,0:T(8,128)(2,1)} %param.7) | copy-start | bytes 2949124
  36.4 70.2 %slice-start = ((s8[4423680]{0:T(1024)(128)(4,1)}), s8[229376]{0:T(1024)(128)(4,1)S(1)}, s32[]{:S(2)}) async-start(s8[4423680]{0:T(1024)(128)(4,1)} %bitcast.25), calls=%async_computation.6 | async-start | bytes 458752
  49.5 6.5 %collective-permute-start = (bf16[384,320]{1,0:T(8,128)(2,1)}, bf16[384,320]{1,0:T(8,128)(2,1)}, u32[]{:S(2)}, u32[]{:S(2)}) collective-permute-start(bf16[384,320]{1,0:T(8,128)(2,1)} %bitcast.11), channel_id=1, source_target_pairs={{0,8},{8,16},{16,24},{24,0},{1,9},{9,17},{17,25},{25,1},{2,10},{10... | collective-permute-start | bytes 737288 | tf_op jit(solution)/shard_map/ppermute | solution.py:251
  55.9 2.3 %copy-start.1 = (bf16[1,2,9,320,320]{4,3,2,1,0:T(8,128)(2,1)S(1)}, bf16[1,2,9,320,320]{4,3,2,1,0:T(8,128)(2,1)}, u32[]{:S(2)}) copy-start(bf16[1,2,9,320,320]{4,3,2,1,0:T(8,128)(2,1)} %param.10) | copy-start | bytes 11059204
  58.2 20.8 %copy-start.6 = (bf16[1,320,320]{2,1,0:T(8,128)(2,1)S(1)}, bf16[1,320,320]{2,1,0:T(8,128)(2,1)}, u32[]{:S(2)}) copy-start(bf16[1,320,320]{2,1,0:T(8,128)(2,1)} %param.13) | copy-start | bytes 614404
  58.2 48.4 %slice-start.1 = ((s8[4423680]{0:T(1024)(128)(4,1)}), s8[4194304]{0:T(1024)(128)(4,1)S(1)}, s32[]{:S(2)}) async-start(s8[4423680]{0:T(1024)(128)(4,1)} %bitcast.25), calls=%async_computation.7 | async-start | bytes 8388608
  100.4 6.1 %collective-permute-start.1 = (bf16[384,320]{1,0:T(8,128)(2,1)S(1)}, bf16[384,320]{1,0:T(8,128)(2,1)S(1)}, u32[]{:S(2)}, u32[]{:S(2)}) collective-permute-start(bf16[384,320]{1,0:T(8,128)(2,1)S(1)} %bitcast.49), channel_id=1, source_target_pairs={{0,8},{8,16},{16,24},{24,0},{1,9},{9,17},{17,25},{25,1},{2,10},{10... | collective-permute-start | bytes 737288 | tf_op jit(solution)/shard_map/ppermute | solution.py:251
where the time goes:
time: 148 us
  blocking collectives  78 us (53%)
  Pallas kernels  49.3 us (33%)
  waiting for transfers between devices  10.6 us (7%)
  local copies, waits for them, and re-layouts  6.11 us (4%)
  other arithmetic  3.49 us (2%)
    all_to_all x3, blocking collectives, shards(): lax.all_to_all(grouped, 'seq', split_axis=0, concat_axis=0, tiled=True)  41.1 us
    all_to_all x3, blocking collectives, shards(): lax.all_to_all(done.reshape(devices, share, channels), 'seq', split_axis=...  36.9 us
    pallas_call x3, Pallas kernels, temporal_part(): pl.pallas_call(functools.partial(temporal_kernel, frames, items), out_sha...  26.7 us
    pallas_call x3, Pallas kernels, spatial_part(): pl.pallas_call(functools.partial(spatial_kernel, height, width, picked is...  22.6 us
    ppermute x2, waiting for transfers between devices, shards(): passed = lax.ppermute(current, 'section', ring)  10.6 us
    unnamed x22, local copies, waits for them, and re-layouts  5.51 us
  transfers between devices with their start and end apart: 2, of which 2 were waited for; matrix products, arithmetic and copies ran while one was open for 1% of the time, Pallas kernels for 0%

commit v1 on v0

--- a/solution.py
+++ b/solution.py
@@ -57,7 +57,7 @@
 
 def spatial_kernel(height, width, picks, *refs):
     if picks:
-        pick_ref, entering_ref, passed_ref, weight_ref, out_ref, kernels, taps, sems = refs
+        _, entering_ref, passed_ref, weight_ref, out_ref, kernels, taps, sems = refs
     else:
         passed_ref, weight_ref, out_ref, kernels, taps, sems = refs
     cells, channels = out_ref.shape
@@ -98,29 +98,29 @@
 
     start = passed_ref[...]
     if picks:
-        start = jnp.where(pick_ref[0] == 1, entering_ref[...], start)
+        start = jnp.where(lax.axis_index("section") == 0, entering_ref[...], start)
     start = start.astype(jnp.float32)
     middle = conv(silu(group_norm(start, same_group)), 0).astype(jnp.bfloat16).astype(jnp.float32)
     after = conv(silu(group_norm(middle, same_group)), 1)
     out_ref[...] = (start + after).astype(jnp.bfloat16)
 
 
-def spatial_part(height, width, passed, weights, picked=None, entering=None):
+def spatial_part(height, width, passed, weights, plan=None, entering=None, turn=0):
     cells, channels = passed.shape
     weights = weights.reshape(2, 3, 3 * channels, weights.shape[-1])
     specs = [
         pl.BlockSpec((cells, channels), lambda i, *_: (0, 0)),
-        pl.BlockSpec(memory_space=pl.ANY),
+        pl.BlockSpec(memory_space=pltpu.HBM),
     ]
     operands = [passed, weights]
-    if picked is not None:
-        specs = [pl.BlockSpec((None, cells, channels), lambda i, pick: (pick[1], 0, 0))] + specs
-        operands = [picked, entering] + operands
+    if plan is not None:
+        specs = [pl.BlockSpec((None, cells, channels), lambda i, order: (order[turn], 0, 0))] + specs
+        operands = [plan, entering] + operands
     return pl.pallas_call(
-        functools.partial(spatial_kernel, height, width, picked is not None),
+        functools.partial(spatial_kernel, height, width, plan is not None),
         out_shape=jax.ShapeDtypeStruct((cells, channels), jnp.bfloat16),
         grid_spec=pltpu.PrefetchScalarGridSpec(
-            num_scalar_prefetch=0 if picked is None else 1,
+            num_scalar_prefetch=0 if plan is None else 1,
             grid=(1,),
             in_specs=specs,
             out_specs=pl.BlockSpec((cells, channels), lambda i, *_: (0, 0)),
@@ -216,7 +216,7 @@
 def temporal_part(frames, items, values, kernels, packed, outward):
     rows, channels = values.shape
     kernels = kernels.reshape(2, 3 * channels, kernels.shape[-1])
-    anywhere = pl.BlockSpec(memory_space=pl.ANY)
+    anywhere = pl.BlockSpec(memory_space=pltpu.HBM)
     return pl.pallas_call(
         functools.partial(temporal_kernel, frames, items),
         out_shape=jax.ShapeDtypeStruct((rows, channels), jnp.bfloat16),
@@ -233,13 +233,32 @@
     )(values, kernels, packed, outward)
 
 
+def assemble_kernel(*refs):
+    *parts, out_ref, sems = refs
+    copies = [pltpu.make_async_copy(part, out_ref.at[i], sems.at[i]) for i, part in enumerate(parts)]
+    for copy in copies:
+        copy.start()
+    for copy in copies:
+        copy.wait()
+
+
+def assembled(parts):
+    return pl.pallas_call(
+        assemble_kernel,
+        out_shape=jax.ShapeDtypeStruct((len(parts),) + parts[0].shape, parts[0].dtype),
+        in_specs=[pl.BlockSpec(memory_space=pl.ANY)] * len(parts),
+        out_specs=pl.BlockSpec(memory_space=pl.ANY),
+        scratch_shapes=[pltpu.SemaphoreType.DMA((len(parts),))],
+        compiler_params=pltpu.CompilerParams(vmem_limit_bytes=MIB),
+    )(*parts)
+
+
 def shards(incoming, plan, waiting, spatial_weight, temporal_weight, attn_in, attn_out):
     clips, _, height, width, channels = incoming.shape
     cells = height * width
     devices = lax.axis_size("seq")
     share = cells // devices
     sections = lax.axis_size("section")
-    first_section = (lax.axis_index("section") == 0).astype(jnp.int32)
     entering = incoming.reshape(clips, cells, channels)
     current = waiting.reshape(cells, channels)
     collected = []
@@ -249,8 +268,7 @@
         else:
             ring = [(i, (i + 1) % sections) for i in range(sections)]
             passed = lax.ppermute(current, "section", ring)
-            picked = jnp.stack([first_section, plan[tick - 1]])
-            after = spatial_part(height, width, passed, spatial_weight[0], picked, entering)
+            after = spatial_part(height, width, passed, spatial_weight[0], plan, entering, tick - 1)
         grouped = after.reshape(devices, share, channels)
         gathered = lax.all_to_all(grouped, "seq", split_axis=0, concat_axis=0, tiled=True)
         done = temporal_part(
@@ -260,8 +278,8 @@
             done.reshape(devices, share, channels), "seq", split_axis=0, concat_axis=0, tiled=True
         )
         current = back.reshape(cells, channels)
-        collected.append(current.reshape(height, width, channels))
-    return jnp.stack(collected)[:, None, None]
+        collected.append(current)
+    return assembled(collected).reshape(TICKS, 1, 1, height, width, channels)
 
 
 def solution(mesh):

time: 148 us -> 145 us (0.980)
  other arithmetic: 3.49 us -> 0 us
  waiting for transfers between devices: 10.6 us -> 12.3 us
  local copies, waits for them, and re-layouts: 6.11 us -> 4.61 us
    broadcast_in_dim x1 -> x0, other arithmetic: 2.06 us -> none  [shards(): return jnp.stack(collected)[:, None, None]]
    ppermute x2, waiting for transfers between devices: 10.6 us -> 12.3 us  [shards(): passed = lax.ppermute(current, 'section', ring)]
    unnamed x22 -> x18, local copies, waits for them, and re-layouts: 5.51 us -> 4.61 us
    pallas_call x3 -> x4, Pallas kernels: 22.6 us -> 22.4 us  [the longest x3 21.4 us: spatial_part(): pl.pallas_call(functools.partial(spatial_kernel, height, width, plan is n...]
  transfers between devices with their start and end apart: 2 -> 2, of which waited for: 2 -> 2; matrix products, arithmetic and copies ran while one was open for 1% -> 0% of each run, Pallas kernels for 0% -> 0%
where the time goes in v1:
time: 145 us; the launch traced here: 144 us
  blocking collectives  77.8 us (54%)
  Pallas kernels  49 us (34%)
  waiting for transfers between devices  12.3 us (8%)
  local copies, waits for them, and re-layouts  4.61 us (3%)
    all_to_all x3, blocking collectives, shards(): lax.all_to_all(grouped, 'seq', split_axis=0, concat_axis=0, tiled=True)  41.1 us
    all_to_all x3, blocking collectives, shards(): lax.all_to_all(done.reshape(devices, share, channels), 'seq', split_axis=...  36.6 us
    pallas_call x3, Pallas kernels, temporal_part(): pl.pallas_call(functools.partial(temporal_kernel, frames, items), out_sha...  26.7 us
    pallas_call x3, Pallas kernels, spatial_part(): pl.pallas_call(functools.partial(spatial_kernel, height, width, plan is n...  21.4 us
    ppermute x2, waiting for transfers between devices, shards(): passed = lax.ppermute(current, 'section', ring)  12.3 us
    unnamed x18, local copies, waits for them, and re-layouts  4.61 us
  transfers between devices with their start and end apart: 2, of which 2 were waited for; matrix products, arithmetic and copies ran while one was open for 0% of the time, Pallas kernels for 0%

profile of v1, /device:TPU:0, one launch (start us, length us, event | category | flops | bytes accessed | tf_op | source)
XLA Modules:
  0.0 144.0 jit_solution(7965501671671373681)
XLA Ops:
  0.0 0.0 copy-start
  0.0 2.3 %copy-done = bf16[1,2,9,320,320]{4,3,2,1,0:T(8,128)(2,1)S(1)} copy-done((bf16[1,2,9,320,320]{4,3,2,1,0:T(8,128)(2,1)S(1)}, bf16[1,2,9,320,320]{4,3,2,1,0:T(8,128)(2,1)}, u32[]{:S(2)}) %copy-start) | copy-done | bytes 3686424
  2.3 0.0 copy-start.7
  2.3 1.0 copy-done.7
  3.2 0.0 copy-start.4
  3.2 0.0 copy-start.6
  3.2 0.0 copy-start.1
  3.2 6.8 %shard_map.73 = bf16[384,320]{1,0:T(8,128)(2,1)S(1)} custom-call(bf16[384,320]{1,0:T(8,128)(2,1)S(1)} %bitcast.49, bf16[2,3,960,320]{3,2,1,0:T(8,128)(2,1)S(1)} %bitcast.21), custom_call_target="tpu_custom_call" | custom-call | tf_op jit(solution)/shard_map/pallas_call | solution.py:119
  10.0 17.4 %all_to_all.30 = bf16[8,48,320]{2,1,0:T(8,128)(2,1)S(1)} all-to-all(bf16[8,48,320]{2,1,0:T(8,128)(2,1)S(1)} %bitcast.43), channel_id=1, replica_groups=mesh['section'=4,'seq'=8] {'seq'}, dimensions={0} | all-to-all | bytes 491520 | tf_op jit(solution)/shard_map/all_to_all | solution.py:273
  27.4 0.0 copy-done.4
  27.4 0.0 copy-done.6
  27.4 1.4 copy-done.2
  28.8 8.9 %shard_map.74 = bf16[384,320]{1,0:T(8,128)(2,1)S(1)} custom-call(bf16[384,320]{1,0:T(8,128)(2,1)S(1)} %bitcast.35, bf16[2,960,320]{2,1,0:T(8,128)(2,1)S(1)} %bitcast.24, bf16[320,960]{1,0:T(8,128)(2,1)S(1)} %bitcast.27, bf16[320,320]{1,0:T(8,128)(2,1)S(1)} %bitcast.32), custom_call_target="tpu_custom_call" | custom-call | tf_op jit(solution)/shard_map/pallas_call | solution.py:220
  37.7 12.8 %all_to_all.31 = bf16[8,48,320]{2,1,0:T(8,128)(2,1)S(1)} all-to-all(bf16[8,48,320]{2,1,0:T(8,128)(2,1)S(1)} %bitcast.36), channel_id=1, replica_groups=mesh['section'=4,'seq'=8] {'seq'}, dimensions={0} | all-to-all | bytes 491520 | tf_op jit(solution)/shard_map/all_to_all | solution.py:277
  50.5 0.0 collective-permute-start
  50.6 6.1 %collective-permute-done.refs_2_ = bf16[384,320]{1,0:T(8,128)(2,1)S(1)} collective-permute-done((bf16[384,320]{1,0:T(8,128)(2,1)S(1)}, bf16[384,320]{1,0:T(8,128)(2,1)S(1)}, u32[]{:S(2)}, u32[]{:S(2)}) %collective-permute-start) | collective-permute-done | bytes 245792 | tf_op jit(solution)/shard_map/ppermute | solution.py:270
  56.7 0.0 copy-done.1
  56.7 0.0 copy-done.5
  56.7 0.0 copy-done.8
  56.7 0.0 copy-start.3
  56.7 7.3 %shard_map.75 = bf16[384,320]{1,0:T(8,128)(2,1)S(1)} custom-call(s32[4]{0:T(128)S(1)} %copy-done.8, bf16[4,384,320]{2,1,0:T(8,128)(2,1)S(1)} %bitcast.30, bf16[384,320]{1,0:T(8,128)(2,1)S(1)} %collective-permute-done.refs_2_, bf16[2,3,960,320]{3,2,1,0:T(8,128)(2,1)S(1)} %bitcast.22), custom_call_target="tpu_custom_call" | custom-call | tf_op jit(solution)/shard_map/pallas_call | solution.py:119
  64.1 12.3 %all_to_all.32 = bf16[8,48,320]{2,1,0:T(8,128)(2,1)S(1)} all-to-all(bf16[8,48,320]{2,1,0:T(8,128)(2,1)S(1)} %bitcast.37), channel_id=1, replica_groups=mesh['section'=4,'seq'=8] {'seq'}, dimensions={0} | all-to-all | bytes 491520 | tf_op jit(solution)/shard_map/all_to_all | solution.py:273
  76.3 0.0 copy-done.3
  76.3 8.9 %shard_map.76 = bf16[384,320]{1,0:T(8,128)(2,1)S(1)} custom-call(bf16[384,320]{1,0:T(8,128)(2,1)S(1)} %bitcast.38, bf16[2,960,320]{2,1,0:T(8,128)(2,1)S(1)} %bitcast.25, bf16[320,960]{1,0:T(8,128)(2,1)S(1)} %bitcast.28, bf16[320,320]{1,0:T(8,128)(2,1)S(1)} %bitcast.33), custom_call_target="tpu_custom_call" | custom-call | tf_op jit(solution)/shard_map/pallas_call | solution.py:220
  85.2 12.5 %all_to_all.33 = bf16[8,48,320]{2,1,0:T(8,128)(2,1)S(1)} all-to-all(bf16[8,48,320]{2,1,0:T(8,128)(2,1)S(1)} %bitcast.39), channel_id=1, replica_groups=mesh['section'=4,'seq'=8] {'seq'}, dimensions={0} | all-to-all | bytes 491520 | tf_op jit(solution)/shard_map/all_to_all | solution.py:277
  97.8 0.0 collective-permute-start.1
  97.8 6.1 %collective-permute-done.1.refs_2_ = bf16[384,320]{1,0:T(8,128)(2,1)S(1)} collective-permute-done((bf16[384,320]{1,0:T(8,128)(2,1)S(1)}, bf16[384,320]{1,0:T(8,128)(2,1)S(1)}, u32[]{:S(2)}, u32[]{:S(2)}) %collective-permute-start.1) | collective-permute-done | bytes 245792 | tf_op jit(solution)/shard_map/ppermute | solution.py:270
  103.9 7.3 %shard_map.77 = bf16[384,320]{1,0:T(8,128)(2,1)S(1)} custom-call(s32[4]{0:T(128)S(1)} %copy-done.8, bf16[4,384,320]{2,1,0:T(8,128)(2,1)S(1)} %bitcast.31, bf16[384,320]{1,0:T(8,128)(2,1)S(1)} %collective-permute-done.1.refs_2_, bf16[2,3,960,320]{3,2,1,0:T(8,128)(2,1)S(1)} %bitcast.23), custom_call_target="tpu_custom_call" | custom-call | tf_op jit(solution)/shard_map/pallas_call | solution.py:119
  111.3 11.4 %all_to_all.34 = bf16[8,48,320]{2,1,0:T(8,128)(2,1)S(1)} all-to-all(bf16[8,48,320]{2,1,0:T(8,128)(2,1)S(1)} %bitcast.40), channel_id=1, replica_groups=mesh['section'=4,'seq'=8] {'seq'}, dimensions={0} | all-to-all | bytes 491520 | tf_op jit(solution)/shard_map/all_to_all | solution.py:273
  122.7 8.9 %shard_map.78 = bf16[384,320]{1,0:T(8,128)(2,1)S(1)} custom-call(bf16[384,320]{1,0:T(8,128)(2,1)S(1)} %bitcast.41, bf16[2,960,320]{2,1,0:T(8,128)(2,1)S(1)} %bitcast.26, bf16[320,960]{1,0:T(8,128)(2,1)S(1)} %bitcast.29, bf16[320,320]{1,0:T(8,128)(2,1)S(1)} %bitcast.34), custom_call_target="tpu_custom_call" | custom-call | tf_op jit(solution)/shard_map/pallas_call | solution.py:220
  131.6 11.3 %all_to_all.35 = bf16[8,48,320]{2,1,0:T(8,128)(2,1)S(1)} all-to-all(bf16[8,48,320]{2,1,0:T(8,128)(2,1)S(1)} %bitcast.42), channel_id=1, replica_groups=mesh['section'=4,'seq'=8] {'seq'}, dimensions={0} | all-to-all | bytes 491520 | tf_op jit(solution)/shard_map/all_to_all | solution.py:277
  142.9 0.9 shard_map.79
  (3 shorter events, 0.0 us)
Async XLA Ops:
  0.0 2.3 %copy-start = (bf16[1,2,9,320,320]{4,3,2,1,0:T(8,128)(2,1)S(1)}, bf16[1,2,9,320,320]{4,3,2,1,0:T(8,128)(2,1)}, u32[]{:S(2)}) copy-start(bf16[1,2,9,320,320]{4,3,2,1,0:T(8,128)(2,1)} %param.10) | copy-start | bytes 11059204
  2.3 1.0 copy-start.7
  3.2 24.2 %copy-start.4 = (bf16[1,320,960]{2,1,0:T(8,128)(2,1)S(1)}, bf16[1,320,960]{2,1,0:T(8,128)(2,1)}, u32[]{:S(2)}) copy-start(bf16[1,320,960]{2,1,0:T(8,128)(2,1)} %param.12) | copy-start | bytes 1843204
  3.2 24.2 %copy-start.6 = (bf16[1,320,320]{2,1,0:T(8,128)(2,1)S(1)}, bf16[1,320,320]{2,1,0:T(8,128)(2,1)}, u32[]{:S(2)}) copy-start(bf16[1,320,320]{2,1,0:T(8,128)(2,1)} %param.13) | copy-start | bytes 614404
  3.2 53.5 %copy-start.1 = (bf16[1,2,9,320,320]{4,3,2,1,0:T(8,128)(2,1)S(1)}, bf16[1,2,9,320,320]{4,3,2,1,0:T(8,128)(2,1)}, u32[]{:S(2)}) copy-start(bf16[1,2,9,320,320]{4,3,2,1,0:T(8,128)(2,1)} %param.10) | copy-start | bytes 11059204
  27.4 1.4 copy-start.2
  28.8 27.9 %copy-start.5 = (bf16[4,1,16,24,320]{4,3,2,1,0:T(8,128)(2,1)S(1)}, bf16[4,1,16,24,320]{4,3,2,1,0:T(8,128)(2,1)}, u32[]{:S(2)}) copy-start(bf16[4,1,16,24,320]{4,3,2,1,0:T(8,128)(2,1)} %param.7) | copy-start | bytes 2949124
  28.8 27.9 %copy-start.8 = (s32[4]{0:T(128)S(1)}, s32[4]{0:T(128)}, u32[]{:S(2)}) copy-start(s32[4]{0:T(128)} %refs_0_.3) | copy-start | bytes 52
  50.5 6.1 %collective-permute-start = (bf16[384,320]{1,0:T(8,128)(2,1)S(1)}, bf16[384,320]{1,0:T(8,128)(2,1)S(1)}, u32[]{:S(2)}, u32[]{:S(2)}) collective-permute-start(bf16[384,320]{1,0:T(8,128)(2,1)S(1)} %bitcast.44), channel_id=1, source_target_pairs={{0,8},{8,16},{16,24},{24,0},{1,9},{9,17},{17,25},{25,1},{2,10},{10... | collective-permute-start | bytes 737288 | tf_op jit(solution)/shard_map/ppermute | solution.py:270
  56.7 19.6 %copy-start.3 = (bf16[1,2,3,320,320]{4,3,2,1,0:T(8,128)(2,1)S(1)}, bf16[1,2,3,320,320]{4,3,2,1,0:T(8,128)(2,1)}, u32[]{:S(2)}) copy-start(bf16[1,2,3,320,320]{4,3,2,1,0:T(8,128)(2,1)} %param.11) | copy-start | bytes 3686404
  97.8 6.1 %collective-permute-start.1 = (bf16[384,320]{1,0:T(8,128)(2,1)S(1)}, bf16[384,320]{1,0:T(8,128)(2,1)S(1)}, u32[]{:S(2)}, u32[]{:S(2)}) collective-permute-start(bf16[384,320]{1,0:T(8,128)(2,1)S(1)} %bitcast.46), channel_id=1, source_target_pairs={{0,8},{8,16},{16,24},{24,0},{1,9},{9,17},{17,25},{25,1},{2,10},{10... | collective-permute-start | bytes 737288 | tf_op jit(solution)/shard_map/ppermute | solution.py:270

commit v2 on v1

--- a/solution.py
+++ b/solution.py
@@ -12,6 +12,8 @@
 TICKS = 3
 EPSILON = 1e-05
 MIB = 1 << 20
+LANES = 128
+LOG2_E = 1.4426950408889634
 
 
 def silu(values):
@@ -48,27 +50,37 @@
     return shifted * lax.rsqrt(spread + EPSILON)
 
 
-def layer_norm(values):
-    center = jnp.mean(values, axis=-1, keepdims=True)
-    shifted = values - center
-    spread = jnp.mean(jnp.square(shifted), axis=-1, keepdims=True)
-    return shifted * lax.rsqrt(spread + EPSILON)
-
-
-def spatial_kernel(height, width, picks, *refs):
+def layer_norm(values, ones):
+    channels = values.shape[-1]
+
+    def across(sums):
+        pieces = -(-channels // sums.shape[-1])
+        return jnp.concatenate([sums] * pieces, axis=-1)[:, :channels]
+
+    floats = values.astype(jnp.float32)
+    center = jnp.dot(values, ones, preferred_element_type=jnp.float32) * (1.0 / channels)
+    shifted = floats - across(center)
+    squares = jnp.square(shifted).astype(jnp.bfloat16)
+    spread = jnp.dot(squares, ones, preferred_element_type=jnp.float32) * (1.0 / channels)
+    return shifted * across(lax.rsqrt(spread + EPSILON))
+
+
+def spatial_kernel(height, width, picks, stream, *refs):
     if picks:
-        _, entering_ref, passed_ref, weight_ref, out_ref, kernels, taps, sems = refs
-    else:
-        passed_ref, weight_ref, out_ref, kernels, taps, sems = refs
+        _, entering_ref, *refs = refs
+    passed_ref, weight_ref, out_ref, taps, *refs = refs
     cells, channels = out_ref.shape
     copies = []
-    for layer in range(2):
-        for row in range(3):
-            copy = pltpu.make_async_copy(
-                weight_ref.at[layer, row], kernels.at[layer, row], sems.at[layer, row]
-            )
-            copy.start()
-            copies.append(copy)
+    kernels = weight_ref
+    if stream:
+        kernels, sems = refs
+        for layer in range(2):
+            for row in range(3):
+                copy = pltpu.make_async_copy(
+                    weight_ref.at[layer, row], kernels.at[layer, row], sems.at[layer, row]
+                )
+                copy.start()
+                copies.append(copy)
     edge = jnp.zeros((width, 3 * channels), jnp.bfloat16)
     taps[0:width, :] = edge
     taps[width + cells : 2 * width + cells, :] = edge
@@ -87,7 +99,8 @@
         taps[width : width + cells, 2 * channels : 3 * channels] = right.astype(jnp.bfloat16)
         total = None
         for row in range(3):
-            copies[3 * layer + row].wait()
+            if stream:
+                copies[3 * layer + row].wait()
             part = jnp.dot(
                 taps[row * width : row * width + cells, :],
                 kernels[layer, row],
@@ -108,42 +121,32 @@
 def spatial_part(height, width, passed, weights, plan=None, entering=None, turn=0):
     cells, channels = passed.shape
     weights = weights.reshape(2, 3, 3 * channels, weights.shape[-1])
+    stream = plan is None
     specs = [
         pl.BlockSpec((cells, channels), lambda i, *_: (0, 0)),
-        pl.BlockSpec(memory_space=pltpu.HBM),
+        pl.BlockSpec(memory_space=pltpu.HBM if stream else pltpu.VMEM),
     ]
     operands = [passed, weights]
     if plan is not None:
         specs = [pl.BlockSpec((None, cells, channels), lambda i, order: (order[turn], 0, 0))] + specs
         operands = [plan, entering] + operands
     return pl.pallas_call(
-        functools.partial(spatial_kernel, height, width, plan is not None),
+        functools.partial(spatial_kernel, height, width, plan is not None, stream),
         out_shape=jax.ShapeDtypeStruct((cells, channels), jnp.bfloat16),
         grid_spec=pltpu.PrefetchScalarGridSpec(
             num_scalar_prefetch=0 if plan is None else 1,
             grid=(1,),
             in_specs=specs,
             out_specs=pl.BlockSpec((cells, channels), lambda i, *_: (0, 0)),
-            scratch_shapes=[
-                pltpu.VMEM(weights.shape, jnp.bfloat16),
-                pltpu.VMEM((cells + 2 * width, 3 * channels), jnp.bfloat16),
-                pltpu.SemaphoreType.DMA((2, 3)),
-            ],
+            scratch_shapes=[pltpu.VMEM((cells + 2 * width, 3 * channels), jnp.bfloat16)]
+            + ([pltpu.VMEM(weights.shape, jnp.bfloat16), pltpu.SemaphoreType.DMA((2, 3))] if stream else []),
         ),
-        compiler_params=pltpu.CompilerParams(vmem_limit_bytes=24 * MIB),
+        compiler_params=pltpu.CompilerParams(vmem_limit_bytes=(58 if stream else 24) * MIB),
     )(*operands)
 
 
-def temporal_kernel(frames, items, in_ref, conv_ref, packed_ref, outward_ref, out_ref, kernels, packed, outward, taps, sems):
+def temporal_kernel(frames, items, in_ref, kernels, packed, outward, out_ref, taps):
     rows, channels = out_ref.shape
-    copies = [
-        pltpu.make_async_copy(conv_ref.at[0], kernels.at[0], sems.at[0]),
-        pltpu.make_async_copy(conv_ref.at[1], kernels.at[1], sems.at[1]),
-        pltpu.make_async_copy(packed_ref, packed, sems.at[2]),
-        pltpu.make_async_copy(outward_ref, outward, sems.at[3]),
-    ]
-    for copy in copies:
-        copy.start()
     aligned = items % 16 == 0
 
     def conv(values, layer):
@@ -162,15 +165,14 @@
             taps[:, 0:channels] = before.astype(jnp.bfloat16)
             taps[:, channels : 2 * channels] = values.astype(jnp.bfloat16)
             taps[:, 2 * channels : 3 * channels] = behind.astype(jnp.bfloat16)
-        copies[layer].wait()
         return jnp.dot(taps[...], kernels[layer], preferred_element_type=jnp.float32)
 
-    start = in_ref[...].astype(jnp.float32)
-    middle = conv(silu(layer_norm(start)), 0).astype(jnp.bfloat16).astype(jnp.float32)
-    after = (start + conv(silu(layer_norm(middle)), 1)).astype(jnp.bfloat16).astype(jnp.float32)
-
-    normed = layer_norm(after).astype(jnp.bfloat16)
-    copies[2].wait()
+    ones = jnp.ones((channels, LANES), jnp.bfloat16)
+    start = in_ref[...]
+    middle = conv(silu(layer_norm(start, ones)), 0).astype(jnp.bfloat16)
+    after = (start.astype(jnp.float32) + conv(silu(layer_norm(middle, ones)), 1)).astype(jnp.bfloat16)
+
+    normed = layer_norm(after, ones).astype(jnp.bfloat16)
     taps[...] = jnp.dot(normed, packed[...], preferred_element_type=jnp.float32).astype(jnp.bfloat16)
     queries = taps[:, 0:channels]
     keys = taps[:, channels : 2 * channels]
@@ -181,53 +183,63 @@
     size = frames * block
     apart = within((size, size), 0, block) != within((size, size), 1, block)
     blocked = jnp.where(apart, -1e30, 0.0)
-    copies[3].wait()
+    scale = head_size ** (-0.5) * LOG2_E
+    groups = [(first, min(first + LANES, channels)) for first in range(0, channels, LANES)]
+    tall = jnp.ones((size, LANES), jnp.bfloat16)
+
+    def part(whole, first):
+        if block == items:
+            return whole
+        return jnp.concatenate(
+            [whole[f * items + first : f * items + first + block] for f in range(frames)], axis=0
+        )
+
     mixed_blocks = []
     for first in range(0, items, block):
-        def part(whole):
-            if block == items:
-                return whole
-            return jnp.concatenate(
-                [whole[f * items + first : f * items + first + block] for f in range(frames)], axis=0
+        q, k, v = part(queries, first), part(keys, first), part(values, first)
+        mixed = []
+        for low, high in groups:
+            heads = (high - low) // head_size
+            owner = bucket((size, high - low), 1, head_size)
+            chosen = q[:, low:high]
+            if heads > 1:
+                chosen = jnp.concatenate(
+                    [jnp.where(owner == head, chosen, jnp.zeros_like(chosen)) for head in range(heads)], axis=0
+                )
+            scores = lax.dot_general(
+                chosen, k[:, low:high], (((1,), (1,)), ((), ())), preferred_element_type=jnp.float32
             )
-
-        q, k, v = part(queries), part(keys), part(values)
-        mixed = []
-        for head in range(HEADS):
-            lanes = slice(head * head_size, (head + 1) * head_size)
-            scores = lax.dot_general(
-                q[:, lanes], k[:, lanes], (((1,), (1,)), ((), ())), preferred_element_type=jnp.float32
-            ) * head_size ** (-0.5) + blocked
+            scores = scores.reshape(heads, size, size) * scale + blocked
             top = jnp.max(scores, axis=-1, keepdims=True)
-            raised = jnp.exp(scores - top)
-            weights = (raised / jnp.sum(raised, axis=-1, keepdims=True)).astype(jnp.bfloat16)
-            mixed.append(jnp.dot(weights, v[:, lanes], preferred_element_type=jnp.float32))
-        mixed_blocks.append(jnp.concatenate(mixed, axis=1).astype(jnp.bfloat16))
+            raised = jnp.exp2(scores - top).astype(jnp.bfloat16).reshape(heads * size, size)
+            both = jnp.dot(raised, jnp.concatenate([tall, v[:, low:high]], axis=1), preferred_element_type=jnp.float32)
+            share = both[:, LANES:] / both[:, : high - low]
+            out = share[0:size]
+            for head in range(1, heads):
+                out = jnp.where(owner == head, share[head * size : (head + 1) * size], out)
+            mixed.append(out.astype(jnp.bfloat16))
+        mixed_blocks.append(jnp.concatenate(mixed, axis=1))
     if len(mixed_blocks) == 1:
         mixed = mixed_blocks[0]
     else:
         mixed = jnp.concatenate(
             [piece[f * block : (f + 1) * block] for f in range(frames) for piece in mixed_blocks], axis=0
         )
-    result = after + jnp.dot(mixed, outward[...], preferred_element_type=jnp.float32)
+    result = after.astype(jnp.float32) + jnp.dot(mixed, outward[...], preferred_element_type=jnp.float32)
     out_ref[...] = result.astype(jnp.bfloat16)
 
 
 def temporal_part(frames, items, values, kernels, packed, outward):
     rows, channels = values.shape
     kernels = kernels.reshape(2, 3 * channels, kernels.shape[-1])
-    anywhere = pl.BlockSpec(memory_space=pltpu.HBM)
+    resident = pl.BlockSpec(memory_space=pltpu.VMEM)
     return pl.pallas_call(
         functools.partial(temporal_kernel, frames, items),
         out_shape=jax.ShapeDtypeStruct((rows, channels), jnp.bfloat16),
-        in_specs=[pl.BlockSpec(memory_space=pltpu.VMEM), anywhere, anywhere, anywhere],
+        in_specs=[resident] * 4,
         out_specs=pl.BlockSpec(memory_space=pltpu.VMEM),
         scratch_shapes=[
-            pltpu.VMEM(kernels.shape, jnp.bfloat16),
-            pltpu.VMEM(packed.shape, jnp.bfloat16),
-            pltpu.VMEM(outward.shape, jnp.bfloat16),
             pltpu.VMEM((rows, 3 * channels), jnp.bfloat16),
-            pltpu.SemaphoreType.DMA((4,)),
         ],
         compiler_params=pltpu.CompilerParams(vmem_limit_bytes=24 * MIB),
     )(values, kernels, packed, outward)

time: 145 us -> 123 us (0.85)
  Pallas kernels: 49 us -> 30.5 us
  local copies, waits for them, and re-layouts: 4.61 us -> 1.4 us
    pallas_call x3, Pallas kernels: 26.7 us -> 12.5 us  [temporal_part(): pl.pallas_call(functools.partial(temporal_kernel, frames, items), out_sha...]
    pallas_call x3, Pallas kernels: 21.4 us -> 17.1 us  [spatial_part(): pl.pallas_call(functools.partial(spatial_kernel, height, width, plan is n...]
    unnamed x18 -> x14, local copies, waits for them, and re-layouts: 4.61 us -> 1.4 us
where the time goes in v2:
time: 123 us; the launch traced here: 122 us
  blocking collectives  78 us (63%)
  Pallas kernels  30.5 us (25%)
  waiting for transfers between devices  12.3 us (10%)
  local copies, waits for them, and re-layouts  1.4 us (1%)
    all_to_all x3, blocking collectives, shards(): lax.all_to_all(grouped, 'seq', split_axis=0, concat_axis=0, tiled=True)  41.3 us
    all_to_all x3, blocking collectives, shards(): lax.all_to_all(done.reshape(devices, share, channels), 'seq', split_axis=...  36.7 us
    pallas_call x3, Pallas kernels, spatial_part(): pl.pallas_call(functools.partial(spatial_kernel, height, width, plan is n...  17.1 us
    pallas_call x3, Pallas kernels, temporal_part(): pl.pallas_call(functools.partial(temporal_kernel, frames, items), out_sha...  12.5 us
    ppermute x2, waiting for transfers between devices, shards(): passed = lax.ppermute(current, 'section', ring)  12.3 us
  transfers between devices with their start and end apart: 2, of which 2 were waited for; matrix products, arithmetic and copies ran while one was open for 0% of the time, Pallas kernels for 0%

profile of v2, /device:TPU:0, one launch (start us, length us, event | category | flops | bytes accessed | tf_op | source)
XLA Modules:
  0.0 122.4 jit_solution(9855563265204845663)
XLA Ops:
  0.0 0.0 copy-start.3
  0.0 0.0 copy-start.5
  0.0 0.0 copy-start
  0.0 7.6 %shard_map.73 = bf16[384,320]{1,0:T(8,128)(2,1)} custom-call(bf16[384,320]{1,0:T(8,128)(2,1)} %bitcast.49, bf16[2,3,960,320]{3,2,1,0:T(8,128)(2,1)} %bitcast.21), custom_call_target="tpu_custom_call" | custom-call | tf_op jit(solution)/shard_map/pallas_call | solution.py:133
  7.7 17.6 %all_to_all.30 = bf16[8,48,320]{2,1,0:T(8,128)(2,1)S(1)} all-to-all(bf16[8,48,320]{2,1,0:T(8,128)(2,1)} %bitcast.48), channel_id=1, replica_groups=mesh['section'=4,'seq'=8] {'seq'}, dimensions={0} | all-to-all | bytes 491520 | tf_op jit(solution)/shard_map/all_to_all | solution.py:285
  25.3 0.0 copy-done.3
  25.3 0.0 copy-done.5
  25.3 0.0 copy-start.1
  25.3 1.4 %copy-done.1 = bf16[1,2,3,320,320]{4,3,2,1,0:T(8,128)(2,1)S(1)} copy-done((bf16[1,2,3,320,320]{4,3,2,1,0:T(8,128)(2,1)S(1)}, bf16[1,2,3,320,320]{4,3,2,1,0:T(8,128)(2,1)}, u32[]{:S(2)}) %copy-start.1) | copy-done | bytes 1228824
  26.7 0.0 copy-start.4
  26.7 0.0 copy-start.6
  26.7 4.2 %shard_map.74 = bf16[384,320]{1,0:T(8,128)(2,1)S(1)} custom-call(bf16[384,320]{1,0:T(8,128)(2,1)S(1)} %bitcast.35, bf16[2,960,320]{2,1,0:T(8,128)(2,1)S(1)} %bitcast.24, bf16[320,960]{1,0:T(8,128)(2,1)S(1)} %bitcast.27, bf16[320,320]{1,0:T(8,128)(2,1)S(1)} %bitcast.32), custom_call_target="tpu_custom_call" | custom-call | tf_op jit(solution)/shard_map/pallas_call | solution.py:236
  30.8 12.8 %all_to_all.31 = bf16[8,48,320]{2,1,0:T(8,128)(2,1)S(1)} all-to-all(bf16[8,48,320]{2,1,0:T(8,128)(2,1)S(1)} %bitcast.36), channel_id=1, replica_groups=mesh['section'=4,'seq'=8] {'seq'}, dimensions={0} | all-to-all | bytes 491520 | tf_op jit(solution)/shard_map/all_to_all | solution.py:289
  43.7 0.0 collective-permute-start
  43.7 6.1 %collective-permute-done.refs_2_ = bf16[384,320]{1,0:T(8,128)(2,1)S(1)} collective-permute-done((bf16[384,320]{1,0:T(8,128)(2,1)S(1)}, bf16[384,320]{1,0:T(8,128)(2,1)S(1)}, u32[]{:S(2)}, u32[]{:S(2)}) %collective-permute-start) | collective-permute-done | bytes 245792 | tf_op jit(solution)/shard_map/ppermute | solution.py:282
  49.8 0.0 copy-done
  49.8 0.0 copy-done.4
  49.8 0.0 copy-done.6
  49.8 0.0 copy-start.2
  49.8 4.7 %shard_map.75 = bf16[384,320]{1,0:T(8,128)(2,1)S(1)} custom-call(s32[4]{0:T(128)S(1)} %copy-done.6, bf16[4,384,320]{2,1,0:T(8,128)(2,1)S(1)} %bitcast.30, bf16[384,320]{1,0:T(8,128)(2,1)S(1)} %collective-permute-done.refs_2_, bf16[2,3,960,320]{3,2,1,0:T(8,128)(2,1)S(1)} %bitcast.22), custom_call_target="tpu_custom_call" | custom-call | tf_op jit(solution)/shard_map/pallas_call | solution.py:133
  54.6 12.3 %all_to_all.32 = bf16[8,48,320]{2,1,0:T(8,128)(2,1)S(1)} all-to-all(bf16[8,48,320]{2,1,0:T(8,128)(2,1)S(1)} %bitcast.37), channel_id=1, replica_groups=mesh['section'=4,'seq'=8] {'seq'}, dimensions={0} | all-to-all | bytes 491520 | tf_op jit(solution)/shard_map/all_to_all | solution.py:285
  66.9 0.0 copy-done.2
  66.9 4.2 %shard_map.76 = bf16[384,320]{1,0:T(8,128)(2,1)S(1)} custom-call(bf16[384,320]{1,0:T(8,128)(2,1)S(1)} %bitcast.38, bf16[2,960,320]{2,1,0:T(8,128)(2,1)S(1)} %bitcast.25, bf16[320,960]{1,0:T(8,128)(2,1)S(1)} %bitcast.28, bf16[320,320]{1,0:T(8,128)(2,1)S(1)} %bitcast.33), custom_call_target="tpu_custom_call" | custom-call | tf_op jit(solution)/shard_map/pallas_call | solution.py:236
  71.0 12.6 %all_to_all.33 = bf16[8,48,320]{2,1,0:T(8,128)(2,1)S(1)} all-to-all(bf16[8,48,320]{2,1,0:T(8,128)(2,1)S(1)} %bitcast.39), channel_id=1, replica_groups=mesh['section'=4,'seq'=8] {'seq'}, dimensions={0} | all-to-all | bytes 491520 | tf_op jit(solution)/shard_map/all_to_all | solution.py:289
  83.6 0.0 collective-permute-start.1
  83.6 6.1 %collective-permute-done.1.refs_2_ = bf16[384,320]{1,0:T(8,128)(2,1)S(1)} collective-permute-done((bf16[384,320]{1,0:T(8,128)(2,1)S(1)}, bf16[384,320]{1,0:T(8,128)(2,1)S(1)}, u32[]{:S(2)}, u32[]{:S(2)}) %collective-permute-start.1) | collective-permute-done | bytes 245792 | tf_op jit(solution)/shard_map/ppermute | solution.py:282
  89.8 4.7 %shard_map.77 = bf16[384,320]{1,0:T(8,128)(2,1)S(1)} custom-call(s32[4]{0:T(128)S(1)} %copy-done.6, bf16[4,384,320]{2,1,0:T(8,128)(2,1)S(1)} %bitcast.31, bf16[384,320]{1,0:T(8,128)(2,1)S(1)} %collective-permute-done.1.refs_2_, bf16[2,3,960,320]{3,2,1,0:T(8,128)(2,1)S(1)} %bitcast.23), custom_call_target="tpu_custom_call" | custom-call | tf_op jit(solution)/shard_map/pallas_call | solution.py:133
  94.5 11.4 %all_to_all.34 = bf16[8,48,320]{2,1,0:T(8,128)(2,1)S(1)} all-to-all(bf16[8,48,320]{2,1,0:T(8,128)(2,1)S(1)} %bitcast.40), channel_id=1, replica_groups=mesh['section'=4,'seq'=8] {'seq'}, dimensions={0} | all-to-all | bytes 491520 | tf_op jit(solution)/shard_map/all_to_all | solution.py:285
  105.9 4.2 %shard_map.78 = bf16[384,320]{1,0:T(8,128)(2,1)S(1)} custom-call(bf16[384,320]{1,0:T(8,128)(2,1)S(1)} %bitcast.41, bf16[2,960,320]{2,1,0:T(8,128)(2,1)S(1)} %bitcast.26, bf16[320,960]{1,0:T(8,128)(2,1)S(1)} %bitcast.29, bf16[320,320]{1,0:T(8,128)(2,1)S(1)} %bitcast.34), custom_call_target="tpu_custom_call" | custom-call | tf_op jit(solution)/shard_map/pallas_call | solution.py:236
  110.1 11.3 %all_to_all.35 = bf16[8,48,320]{2,1,0:T(8,128)(2,1)S(1)} all-to-all(bf16[8,48,320]{2,1,0:T(8,128)(2,1)S(1)} %bitcast.42), channel_id=1, replica_groups=mesh['section'=4,'seq'=8] {'seq'}, dimensions={0} | all-to-all | bytes 491520 | tf_op jit(solution)/shard_map/all_to_all | solution.py:289
  121.3 0.9 shard_map.79
Async XLA Ops:
  0.0 25.3 %copy-start.3 = (bf16[1,320,960]{2,1,0:T(8,128)(2,1)S(1)}, bf16[1,320,960]{2,1,0:T(8,128)(2,1)}, u32[]{:S(2)}) copy-start(bf16[1,320,960]{2,1,0:T(8,128)(2,1)} %param.12) | copy-start | bytes 1843204
  0.0 25.3 %copy-start.5 = (bf16[1,320,320]{2,1,0:T(8,128)(2,1)S(1)}, bf16[1,320,320]{2,1,0:T(8,128)(2,1)}, u32[]{:S(2)}) copy-start(bf16[1,320,320]{2,1,0:T(8,128)(2,1)} %param.13) | copy-start | bytes 614404
  0.0 49.8 %copy-start = (bf16[1,2,9,320,320]{4,3,2,1,0:T(8,128)(2,1)S(1)}, bf16[1,2,9,320,320]{4,3,2,1,0:T(8,128)(2,1)}, u32[]{:S(2)}) copy-start(bf16[1,2,9,320,320]{4,3,2,1,0:T(8,128)(2,1)} %param.10) | copy-start | bytes 11059204
  25.3 1.4 %copy-start.1 = (bf16[1,2,3,320,320]{4,3,2,1,0:T(8,128)(2,1)S(1)}, bf16[1,2,3,320,320]{4,3,2,1,0:T(8,128)(2,1)}, u32[]{:S(2)}) copy-start(bf16[1,2,3,320,320]{4,3,2,1,0:T(8,128)(2,1)} %param.11) | copy-start | bytes 3686404
  26.7 23.2 %copy-start.4 = (bf16[4,1,16,24,320]{4,3,2,1,0:T(8,128)(2,1)S(1)}, bf16[4,1,16,24,320]{4,3,2,1,0:T(8,128)(2,1)}, u32[]{:S(2)}) copy-start(bf16[4,1,16,24,320]{4,3,2,1,0:T(8,128)(2,1)} %param.7) | copy-start | bytes 2949124
  26.7 23.2 %copy-start.6 = (s32[4]{0:T(128)S(1)}, s32[4]{0:T(128)}, u32[]{:S(2)}) copy-start(s32[4]{0:T(128)} %refs_0_.3) | copy-start | bytes 52
  43.7 6.1 %collective-permute-start = (bf16[384,320]{1,0:T(8,128)(2,1)S(1)}, bf16[384,320]{1,0:T(8,128)(2,1)S(1)}, u32[]{:S(2)}, u32[]{:S(2)}) collective-permute-start(bf16[384,320]{1,0:T(8,128)(2,1)S(1)} %bitcast.43), channel_id=1, source_target_pairs={{0,8},{8,16},{16,24},{24,0},{1,9},{9,17},{17,25},{25,1},{2,10},{10... | collective-permute-start | bytes 737288 | tf_op jit(solution)/shard_map/ppermute | solution.py:282
  49.8 17.0 %copy-start.2 = (bf16[1,2,3,320,320]{4,3,2,1,0:T(8,128)(2,1)S(1)}, bf16[1,2,3,320,320]{4,3,2,1,0:T(8,128)(2,1)}, u32[]{:S(2)}) copy-start(bf16[1,2,3,320,320]{4,3,2,1,0:T(8,128)(2,1)} %param.11) | copy-start | bytes 3686404
  83.6 6.1 %collective-permute-start.1 = (bf16[384,320]{1,0:T(8,128)(2,1)S(1)}, bf16[384,320]{1,0:T(8,128)(2,1)S(1)}, u32[]{:S(2)}, u32[]{:S(2)}) collective-permute-start(bf16[384,320]{1,0:T(8,128)(2,1)S(1)} %bitcast.45), channel_id=1, source_target_pairs={{0,8},{8,16},{16,24},{24,0},{1,9},{9,17},{17,25},{25,1},{2,10},{10... | collective-permute-start | bytes 737288 | tf_op jit(solution)/shard_map/ppermute | solution.py:282

commit v3 on v2

--- a/solution.py
+++ b/solution.py
@@ -29,6 +29,47 @@
 def within(shape, dim, size):
     index = lax.broadcasted_iota(jnp.int32, shape, dim).astype(jnp.float32)
     return index - size * jnp.floor((index + 0.5) * (1.0 / size))
+
+
+def chunk_shape(share, channels):
+    if share % 16 == 0 and channels % LANES * 2 == LANES:
+        return (share * channels // LANES, LANES)
+    return (share, channels)
+
+
+def pack(out_ref, values):
+    devices, height, width = out_ref.shape
+    rows, channels = values.shape
+    share = rows // devices
+    if width == channels:
+        out_ref[...] = values.astype(jnp.bfloat16).reshape(out_ref.shape)
+        return
+    columns = channels // LANES
+    for device in range(devices):
+        own = values[device * share : (device + 1) * share]
+        for column in range(columns):
+            piece = own[:, column * LANES : (column + 1) * LANES]
+            out_ref[device, column * share : (column + 1) * share, :] = piece.astype(jnp.bfloat16)
+        last = own[:, columns * LANES :]
+        piece = jnp.concatenate([last[: share // 2], last[share // 2 :]], axis=1)
+        out_ref[device, columns * share :, :] = piece.astype(jnp.bfloat16)
+
+
+def unpack(in_ref, channels):
+    devices, height, width = in_ref.shape
+    if width == channels:
+        return in_ref[...].astype(jnp.float32).reshape(devices * height, channels)
+    share = height * width // channels
+    columns = channels // LANES
+    rows = []
+    for device in range(devices):
+        pieces = [
+            in_ref[device, column * share : (column + 1) * share, :].astype(jnp.float32) for column in range(columns)
+        ]
+        last = in_ref[device, columns * share :, :].astype(jnp.float32)
+        pieces.append(jnp.concatenate([last[:, : LANES // 2], last[:, LANES // 2 :]], axis=0))
+        rows.append(jnp.concatenate(pieces, axis=1))
+    return jnp.concatenate(rows, axis=0)
 
 
 def group_total(partial, same_group):
@@ -69,7 +110,7 @@
     if picks:
         _, entering_ref, *refs = refs
     passed_ref, weight_ref, out_ref, taps, *refs = refs
-    cells, channels = out_ref.shape
+    cells, channels = height * width, weight_ref.shape[-1]
     copies = []
     kernels = weight_ref
     if stream:
@@ -109,21 +150,23 @@
             total = part if total is None else total + part
         return total
 
-    start = passed_ref[...]
     if picks:
-        start = jnp.where(lax.axis_index("section") == 0, entering_ref[...], start)
-    start = start.astype(jnp.float32)
+        entering = entering_ref[...].astype(jnp.float32)
+        start = jnp.where(lax.axis_index("section") == 0, entering, unpack(passed_ref, channels))
+    else:
+        start = passed_ref[...].astype(jnp.float32)
     middle = conv(silu(group_norm(start, same_group)), 0).astype(jnp.bfloat16).astype(jnp.float32)
     after = conv(silu(group_norm(middle, same_group)), 1)
-    out_ref[...] = (start + after).astype(jnp.bfloat16)
-
-
-def spatial_part(height, width, passed, weights, plan=None, entering=None, turn=0):
-    cells, channels = passed.shape
+    pack(out_ref, start + after)
+
+
+def spatial_part(height, width, devices, passed, weights, plan=None, entering=None, turn=0):
+    cells, channels = height * width, weights.shape[-1]
+    chunks = (devices,) + chunk_shape(cells // devices, channels)
     weights = weights.reshape(2, 3, 3 * channels, weights.shape[-1])
     stream = plan is None
     specs = [
-        pl.BlockSpec((cells, channels), lambda i, *_: (0, 0)),
+        pl.BlockSpec(passed.shape, lambda i, *_: (0,) * passed.ndim),
         pl.BlockSpec(memory_space=pltpu.HBM if stream else pltpu.VMEM),
     ]
     operands = [passed, weights]
@@ -132,21 +175,21 @@
         operands = [plan, entering] + operands
     return pl.pallas_call(
         functools.partial(spatial_kernel, height, width, plan is not None, stream),
-        out_shape=jax.ShapeDtypeStruct((cells, channels), jnp.bfloat16),
+        out_shape=jax.ShapeDtypeStruct(chunks, jnp.bfloat16),
         grid_spec=pltpu.PrefetchScalarGridSpec(
             num_scalar_prefetch=0 if plan is None else 1,
             grid=(1,),
             in_specs=specs,
-            out_specs=pl.BlockSpec((cells, channels), lambda i, *_: (0, 0)),
+            out_specs=pl.BlockSpec(chunks, lambda i, *_: (0, 0, 0)),
             scratch_shapes=[pltpu.VMEM((cells + 2 * width, 3 * channels), jnp.bfloat16)]
             + ([pltpu.VMEM(weights.shape, jnp.bfloat16), pltpu.SemaphoreType.DMA((2, 3))] if stream else []),
         ),
-        compiler_params=pltpu.CompilerParams(vmem_limit_bytes=(58 if stream else 24) * MIB),
+        compiler_params=pltpu.CompilerParams(vmem_limit_bytes=(52 if stream else 24) * MIB),
     )(*operands)
 
 
 def temporal_kernel(frames, items, in_ref, kernels, packed, outward, out_ref, taps):
-    rows, channels = out_ref.shape
+    rows, channels = frames * items, outward.shape[-1]
     aligned = items % 16 == 0
 
     def conv(values, layer):
@@ -168,9 +211,9 @@
         return jnp.dot(taps[...], kernels[layer], preferred_element_type=jnp.float32)
 
     ones = jnp.ones((channels, LANES), jnp.bfloat16)
-    start = in_ref[...]
-    middle = conv(silu(layer_norm(start, ones)), 0).astype(jnp.bfloat16)
-    after = (start.astype(jnp.float32) + conv(silu(layer_norm(middle, ones)), 1)).astype(jnp.bfloat16)
+    start = unpack(in_ref, channels)
+    middle = conv(silu(layer_norm(start.astype(jnp.bfloat16), ones)), 0).astype(jnp.bfloat16)
+    after = (start + conv(silu(layer_norm(middle, ones)), 1)).astype(jnp.bfloat16)
 
     normed = layer_norm(after, ones).astype(jnp.bfloat16)
     taps[...] = jnp.dot(normed, packed[...], preferred_element_type=jnp.float32).astype(jnp.bfloat16)
@@ -226,16 +269,16 @@
             [piece[f * block : (f + 1) * block] for f in range(frames) for piece in mixed_blocks], axis=0
         )
     result = after.astype(jnp.float32) + jnp.dot(mixed, outward[...], preferred_element_type=jnp.float32)
-    out_ref[...] = result.astype(jnp.bfloat16)
+    pack(out_ref, result)
 
 
 def temporal_part(frames, items, values, kernels, packed, outward):
-    rows, channels = values.shape
+    rows, channels = frames * items, outward.shape[-1]
     kernels = kernels.reshape(2, 3 * channels, kernels.shape[-1])
     resident = pl.BlockSpec(memory_space=pltpu.VMEM)
     return pl.pallas_call(
         functools.partial(temporal_kernel, frames, items),
-        out_shape=jax.ShapeDtypeStruct((rows, channels), jnp.bfloat16),
+        out_shape=jax.ShapeDtypeStruct(values.shape, jnp.bfloat16),
         in_specs=[resident] * 4,
         out_specs=pl.BlockSpec(memory_space=pltpu.VMEM),
         scratch_shapes=[
@@ -245,24 +288,26 @@
     )(values, kernels, packed, outward)
 
 
-def assemble_kernel(*refs):
-    *parts, out_ref, sems = refs
-    copies = [pltpu.make_async_copy(part, out_ref.at[i], sems.at[i]) for i, part in enumerate(parts)]
-    for copy in copies:
-        copy.start()
-    for copy in copies:
-        copy.wait()
-
-
-def assembled(parts):
+def collect_kernel(tick, *refs):
+    in_ref, *_, out_ref, rows, sem = refs
+    rows[...] = unpack(in_ref, rows.shape[-1]).astype(jnp.bfloat16)
+    copy = pltpu.make_async_copy(rows, out_ref.at[tick], sem)
+    copy.start()
+    copy.wait()
+
+
+def collect(tick, values, shape, outputs=None):
+    before = [] if outputs is None else [outputs]
     return pl.pallas_call(
-        assemble_kernel,
-        out_shape=jax.ShapeDtypeStruct((len(parts),) + parts[0].shape, parts[0].dtype),
-        in_specs=[pl.BlockSpec(memory_space=pl.ANY)] * len(parts),
+        functools.partial(collect_kernel, tick),
+        out_shape=jax.ShapeDtypeStruct(shape, values.dtype),
+        in_specs=[pl.BlockSpec(memory_space=pltpu.VMEM)] + [pl.BlockSpec(memory_space=pl.ANY)] * len(before),
         out_specs=pl.BlockSpec(memory_space=pl.ANY),
-        scratch_shapes=[pltpu.SemaphoreType.DMA((len(parts),))],
-        compiler_params=pltpu.CompilerParams(vmem_limit_bytes=MIB),
-    )(*parts)
+        scratch_shapes=[pltpu.VMEM(shape[1:], values.dtype), pltpu.SemaphoreType.DMA],
+        input_output_aliases={1: 0} if before else {},
+        compiler_params=pltpu.CompilerParams(vmem_limit_bytes=4 * MIB),
+        cost_estimate=pl.CostEstimate(flops=0, bytes_accessed=4 * values.size, transcendentals=0),
+    )(values, *before)
 
 
 def shards(incoming, plan, waiting, spatial_weight, temporal_weight, attn_in, attn_out):
@@ -273,25 +318,19 @@
     sections = lax.axis_size("section")
     entering = incoming.reshape(clips, cells, channels)
     current = waiting.reshape(cells, channels)
-    collected = []
+    ring = [(i, (i + 1) % sections) for i in range(sections)]
+    outputs = None
     for tick in range(TICKS):
         if tick == 0:
-            after = spatial_part(height, width, current, spatial_weight[0])
+            after = spatial_part(height, width, devices, current, spatial_weight[0])
         else:
-            ring = [(i, (i + 1) % sections) for i in range(sections)]
             passed = lax.ppermute(current, "section", ring)
-            after = spatial_part(height, width, passed, spatial_weight[0], plan, entering, tick - 1)
-        grouped = after.reshape(devices, share, channels)
-        gathered = lax.all_to_all(grouped, "seq", split_axis=0, concat_axis=0, tiled=True)
-        done = temporal_part(
-            devices, share, gathered.reshape(devices * share, channels), temporal_weight[0], attn_in[0], attn_out[0]
-        )
-        back = lax.all_to_all(
-            done.reshape(devices, share, channels), "seq", split_axis=0, concat_axis=0, tiled=True
-        )
-        current = back.reshape(cells, channels)
-        collected.append(current)
-    return assembled(collected).reshape(TICKS, 1, 1, height, width, channels)
+            after = spatial_part(height, width, devices, passed, spatial_weight[0], plan, entering, tick - 1)
+        gathered = lax.all_to_all(after, "seq", split_axis=0, concat_axis=0, tiled=True)
+        done = temporal_part(devices, share, gathered, temporal_weight[0], attn_in[0], attn_out[0])
+        current = lax.all_to_all(done, "seq", split_axis=0, concat_axis=0, tiled=True)
+        outputs = collect(tick, current, (TICKS, cells, channels), outputs)
+    return outputs.reshape(TICKS, 1, 1, height, width, channels)
 
 
 def solution(mesh):

time: 123 us -> 117 us (0.951)
  blocking collectives: 78 us -> 61.3 us
  waiting for transfers between devices: 12.3 us -> 17.7 us
  starting transfers between devices: 0.01 us -> 3.41 us
    all_to_all x6 -> x5, blocking collectives: 78 us -> 61.3 us  [the longest x3 38.4 us: shards(): lax.all_to_all(after, 'seq', split_axis=0, concat_axis=0, tiled=True)]
    all_to_all x0 -> x1, waiting for transfers between devices: none -> 6.42 us  [shards(): lax.all_to_all(done, 'seq', split_axis=0, concat_axis=0, tiled=True)]
    all_to_all x0 -> x1, starting transfers between devices: none -> 3.41 us  [shards(): lax.all_to_all(done, 'seq', split_axis=0, concat_axis=0, tiled=True)]
    pallas_call x3, Pallas kernels: 17.1 us -> 15.2 us  [spatial_part(): pl.pallas_call(functools.partial(spatial_kernel, height, width, plan is n...]
    pallas_call x1 -> x3, Pallas kernels: 0.93 us -> 2.42 us  [collect(): pl.pallas_call(functools.partial(collect_kernel, tick), out_shape=jax.Sha...]
  transfers between devices with their start and end apart: 2 -> 3, of which waited for: 2 -> 3; matrix products, arithmetic and copies ran while one was open for 0% -> 0% of each run, Pallas kernels for 0% -> 1%
where the time goes in v3:
time: 117 us; the launch traced here: 116 us
  blocking collectives  61.3 us (52%)
  Pallas kernels  31.2 us (27%)
  waiting for transfers between devices  17.7 us (15%)
  starting transfers between devices  3.41 us (3%)
  local copies, waits for them, and re-layouts  2.36 us (2%)
    all_to_all x3, blocking collectives, shards(): lax.all_to_all(after, 'seq', split_axis=0, concat_axis=0, tiled=True)  38.4 us
    all_to_all x2, blocking collectives, shards(): lax.all_to_all(done, 'seq', split_axis=0, concat_axis=0, tiled=True)  22.9 us
    pallas_call x3, Pallas kernels, spatial_part(): pl.pallas_call(functools.partial(spatial_kernel, height, width, plan is n...  15.2 us
    pallas_call x3, Pallas kernels, temporal_part(): pl.pallas_call(functools.partial(temporal_kernel, frames, items), out_sha...  13.5 us
    ppermute x2, waiting for transfers between devices, shards(): passed = lax.ppermute(current, 'section', ring)  11.2 us
    all_to_all x1, waiting for transfers between devices, shards(): lax.all_to_all(done, 'seq', split_axis=0, concat_axis=0, tiled=True)  6.42 us
    all_to_all x1, starting transfers between devices, shards(): lax.all_to_all(done, 'seq', split_axis=0, concat_axis=0, tiled=True)  3.41 us
    pallas_call x3, Pallas kernels, collect(): pl.pallas_call(functools.partial(collect_kernel, tick), out_shape=jax.Sha...  2.42 us
  transfers between devices with their start and end apart: 3, of which 3 were waited for; matrix products, arithmetic and copies ran while one was open for 0% of the time, Pallas kernels for 1%

profile of v3, /device:TPU:0, one launch (start us, length us, event | category | flops | bytes accessed | tf_op | source)
XLA Modules:
  0.0 116.1 jit_solution(7900838231562547728)
XLA Ops:
  0.0 0.0 copy-start.6
  0.0 1.0 copy-done.6
  1.0 0.0 copy-start.3
  1.0 0.0 copy-start.5
  1.0 5.5 %shard_map.73 = bf16[8,120,128]{2,1,0:T(8,128)(2,1)S(1)} custom-call(bf16[384,320]{1,0:T(8,128)(2,1)S(1)} %bitcast.23, bf16[2,3,960,320]{3,2,1,0:T(8,128)(2,1)} %bitcast.9), custom_call_target="tpu_custom_call" | custom-call | tf_op jit(solution)/shard_map/pallas_call | solution.py:176
  6.5 15.8 %all_to_all.30.in_ref = bf16[8,120,128]{2,1,0:T(8,128)(2,1)S(1)} all-to-all(bf16[8,120,128]{2,1,0:T(8,128)(2,1)S(1)} %shard_map.73), channel_id=1, replica_groups=mesh['section'=4,'seq'=8] {'seq'}, dimensions={0} | all-to-all | bytes 491520 | tf_op jit(solution)/shard_map/all_to_all | solution.py:329
  22.2 0.0 copy-done.3
  22.2 0.0 copy-done.5
  22.2 1.4 %copy-done.1 = bf16[1,2,3,320,320]{4,3,2,1,0:T(8,128)(2,1)S(1)} copy-done((bf16[1,2,3,320,320]{4,3,2,1,0:T(8,128)(2,1)S(1)}, bf16[1,2,3,320,320]{4,3,2,1,0:T(8,128)(2,1)}, u32[]{:S(2)}) %copy-start.1) | copy-done | bytes 1228824
  23.6 4.3 %shard_map.74 = bf16[8,120,128]{2,1,0:T(8,128)(2,1)S(1)} custom-call(bf16[8,120,128]{2,1,0:T(8,128)(2,1)S(1)} %all_to_all.30.in_ref, bf16[2,960,320]{2,1,0:T(8,128)(2,1)S(1)} %bitcast.12, bf16[320,960]{1,0:T(8,128)(2,1)S(1)} %bitcast.15, bf16[320,320]{1,0:T(8,128)(2,1)S(1)} %bitcast.20), custom_call_target="tpu_custom_call" | custom-call | tf_op jit(solution)/shard_map/pallas_call | solution.py:279
  27.9 11.6 %all_to_all.31.refs_0_ = bf16[8,120,128]{2,1,0:T(8,128)(2,1)S(1)} all-to-all(bf16[8,120,128]{2,1,0:T(8,128)(2,1)S(1)} %shard_map.74), channel_id=1, replica_groups=mesh['section'=4,'seq'=8] {'seq'}, dimensions={0} | all-to-all | bytes 491520 | tf_op jit(solution)/shard_map/all_to_all | solution.py:331
  39.5 0.0 collective-permute-start
  39.5 5.6 %collective-permute-done.refs_2_ = bf16[8,120,128]{2,1,0:T(8,128)(2,1)S(1)} collective-permute-done((bf16[8,120,128]{2,1,0:T(8,128)(2,1)S(1)}, bf16[8,120,128]{2,1,0:T(8,128)(2,1)S(1)}, u32[]{:S(2)}, u32[]{:S(2)}) %collective-permute-start) | collective-permute-done | bytes 245792 | tf_op jit(solution)/shard_map/ppermute | solution.py:327
  45.1 0.0 copy-done
  45.1 0.0 copy-done.4
  45.1 0.0 copy-done.7
  45.2 0.0 copy-start.2
  45.2 4.9 %shard_map.75 = bf16[8,120,128]{2,1,0:T(8,128)(2,1)S(1)} custom-call(s32[4]{0:T(128)S(1)} %copy-done.7, bf16[4,384,320]{2,1,0:T(8,128)(2,1)S(1)} %bitcast.18, bf16[8,120,128]{2,1,0:T(8,128)(2,1)S(1)} %collective-permute-done.refs_2_, bf16[2,3,960,320]{3,2,1,0:T(8,128)(2,1)S(1)} %bitcast.10), custom_call_target="tpu_custom_call" | custom-call | tf_op jit(solution)/shard_map/pallas_call | solution.py:176
  50.0 11.4 %all_to_all.32.in_ref = bf16[8,120,128]{2,1,0:T(8,128)(2,1)S(1)} all-to-all(bf16[8,120,128]{2,1,0:T(8,128)(2,1)S(1)} %shard_map.75), channel_id=1, replica_groups=mesh['section'=4,'seq'=8] {'seq'}, dimensions={0} | all-to-all | bytes 491520 | tf_op jit(solution)/shard_map/all_to_all | solution.py:329
  61.4 0.0 copy-done.2
  61.4 4.3 %shard_map.76 = bf16[8,120,128]{2,1,0:T(8,128)(2,1)S(1)} custom-call(bf16[8,120,128]{2,1,0:T(8,128)(2,1)S(1)} %all_to_all.32.in_ref, bf16[2,960,320]{2,1,0:T(8,128)(2,1)S(1)} %bitcast.13, bf16[320,960]{1,0:T(8,128)(2,1)S(1)} %bitcast.16, bf16[320,320]{1,0:T(8,128)(2,1)S(1)} %bitcast.21), custom_call_target="tpu_custom_call" | custom-call | tf_op jit(solution)/shard_map/pallas_call | solution.py:279
  65.7 11.3 %all_to_all.33.refs_0_ = bf16[8,120,128]{2,1,0:T(8,128)(2,1)S(1)} all-to-all(bf16[8,120,128]{2,1,0:T(8,128)(2,1)S(1)} %shard_map.76), channel_id=1, replica_groups=mesh['section'=4,'seq'=8] {'seq'}, dimensions={0} | all-to-all | bytes 491520 | tf_op jit(solution)/shard_map/all_to_all | solution.py:331
  76.9 0.0 collective-permute-start.1
  77.0 5.6 %collective-permute-done.1.refs_2_ = bf16[8,120,128]{2,1,0:T(8,128)(2,1)S(1)} collective-permute-done((bf16[8,120,128]{2,1,0:T(8,128)(2,1)S(1)}, bf16[8,120,128]{2,1,0:T(8,128)(2,1)S(1)}, u32[]{:S(2)}, u32[]{:S(2)}) %collective-permute-start.1) | collective-permute-done | bytes 245792 | tf_op jit(solution)/shard_map/ppermute | solution.py:327
  82.6 4.9 %shard_map.77 = bf16[8,120,128]{2,1,0:T(8,128)(2,1)S(1)} custom-call(s32[4]{0:T(128)S(1)} %copy-done.7, bf16[4,384,320]{2,1,0:T(8,128)(2,1)S(1)} %bitcast.19, bf16[8,120,128]{2,1,0:T(8,128)(2,1)S(1)} %collective-permute-done.1.refs_2_, bf16[2,3,960,320]{3,2,1,0:T(8,128)(2,1)S(1)} %bitcast.11), custom_call_target="tpu_custom_call" | custom-call | tf_op jit(solution)/shard_map/pallas_call | solution.py:176
  87.4 11.3 %all_to_all.34.in_ref = bf16[8,120,128]{2,1,0:T(8,128)(2,1)S(1)} all-to-all(bf16[8,120,128]{2,1,0:T(8,128)(2,1)S(1)} %shard_map.77), channel_id=1, replica_groups=mesh['section'=4,'seq'=8] {'seq'}, dimensions={0} | all-to-all | bytes 491520 | tf_op jit(solution)/shard_map/all_to_all | solution.py:329
  98.7 5.0 %shard_map.78 = bf16[8,120,128]{2,1,0:T(8,128)(2,1)} custom-call(bf16[8,120,128]{2,1,0:T(8,128)(2,1)S(1)} %all_to_all.34.in_ref, bf16[2,960,320]{2,1,0:T(8,128)(2,1)S(1)} %bitcast.14, bf16[320,960]{1,0:T(8,128)(2,1)S(1)} %bitcast.17, bf16[320,320]{1,0:T(8,128)(2,1)S(1)} %bitcast.22), custom_call_target="tpu_custom_call" | custom-call | tf_op jit(solution)/shard_map/pallas_call | solution.py:279
  103.7 3.4 %all-to-all-start.5 = ((bf16[8,120,128]{2,1,0:T(8,128)(2,1)}), bf16[8,120,128]{2,1,0:T(8,128)(2,1)S(1)}, u32[]{:S(2)}, u32[]{:S(2)}) async-start(bf16[8,120,128]{2,1,0:T(8,128)(2,1)} %shard_map.78), calls=%async_computation.5 | async-start | bytes 491520 | tf_op jit(solution)/shard_map/all_to_all | solution.py:331
  107.1 0.8 shard_map.79.refs_1_
  107.9 0.8 shard_map.80.refs_1_
  108.7 6.4 %all-to-all-done.5.refs_0_ = bf16[8,120,128]{2,1,0:T(8,128)(2,1)S(1)} async-done(((bf16[8,120,128]{2,1,0:T(8,128)(2,1)}), bf16[8,120,128]{2,1,0:T(8,128)(2,1)S(1)}, u32[]{:S(2)}, u32[]{:S(2)}) %all-to-all-start.5) | async-done | bytes 245792 | tf_op jit(solution)/shard_map/all_to_all | solution.py:331
  115.2 0.8 shard_map.81
  (4 shorter events, 0.0 us)
Async XLA Ops:
  0.0 1.0 copy-start.6
  1.0 21.3 %copy-start.3 = (bf16[1,320,960]{2,1,0:T(8,128)(2,1)S(1)}, bf16[1,320,960]{2,1,0:T(8,128)(2,1)}, u32[]{:S(2)}) copy-start(bf16[1,320,960]{2,1,0:T(8,128)(2,1)} %param.12) | copy-start | bytes 1843204
  1.0 21.3 %copy-start.5 = (bf16[1,320,320]{2,1,0:T(8,128)(2,1)S(1)}, bf16[1,320,320]{2,1,0:T(8,128)(2,1)}, u32[]{:S(2)}) copy-start(bf16[1,320,320]{2,1,0:T(8,128)(2,1)} %param.13) | copy-start | bytes 614404
  1.0 44.2 %copy-start = (bf16[1,2,9,320,320]{4,3,2,1,0:T(8,128)(2,1)S(1)}, bf16[1,2,9,320,320]{4,3,2,1,0:T(8,128)(2,1)}, u32[]{:S(2)}) copy-start(bf16[1,2,9,320,320]{4,3,2,1,0:T(8,128)(2,1)} %param.10) | copy-start | bytes 11059204
  22.2 1.4 %copy-start.1 = (bf16[1,2,3,320,320]{4,3,2,1,0:T(8,128)(2,1)S(1)}, bf16[1,2,3,320,320]{4,3,2,1,0:T(8,128)(2,1)}, u32[]{:S(2)}) copy-start(bf16[1,2,3,320,320]{4,3,2,1,0:T(8,128)(2,1)} %param.11) | copy-start | bytes 3686404
  23.6 21.5 %copy-start.4 = (bf16[4,1,16,24,320]{4,3,2,1,0:T(8,128)(2,1)S(1)}, bf16[4,1,16,24,320]{4,3,2,1,0:T(8,128)(2,1)}, u32[]{:S(2)}) copy-start(bf16[4,1,16,24,320]{4,3,2,1,0:T(8,128)(2,1)} %param.7) | copy-start | bytes 2949124
  23.6 21.5 %copy-start.7 = (s32[4]{0:T(128)S(1)}, s32[4]{0:T(128)}, u32[]{:S(2)}) copy-start(s32[4]{0:T(128)} %refs_0_.3) | copy-start | bytes 52
  39.5 5.6 %collective-permute-start = (bf16[8,120,128]{2,1,0:T(8,128)(2,1)S(1)}, bf16[8,120,128]{2,1,0:T(8,128)(2,1)S(1)}, u32[]{:S(2)}, u32[]{:S(2)}) collective-permute-start(bf16[8,120,128]{2,1,0:T(8,128)(2,1)S(1)} %all_to_all.31.refs_0_), channel_id=1, source_target_pairs={{0,8},{8,16},{16,24},{24,0},{1,9},{9,17},{17,25},{25,1},{2,10},{10... | collective-permute-start | bytes 737288 | tf_op jit(solution)/shard_map/ppermute | solution.py:327
  45.2 16.3 %copy-start.2 = (bf16[1,2,3,320,320]{4,3,2,1,0:T(8,128)(2,1)S(1)}, bf16[1,2,3,320,320]{4,3,2,1,0:T(8,128)(2,1)}, u32[]{:S(2)}) copy-start(bf16[1,2,3,320,320]{4,3,2,1,0:T(8,128)(2,1)} %param.11) | copy-start | bytes 3686404
  76.9 5.6 %collective-permute-start.1 = (bf16[8,120,128]{2,1,0:T(8,128)(2,1)S(1)}, bf16[8,120,128]{2,1,0:T(8,128)(2,1)S(1)}, u32[]{:S(2)}, u32[]{:S(2)}) collective-permute-start(bf16[8,120,128]{2,1,0:T(8,128)(2,1)S(1)} %all_to_all.33.refs_0_), channel_id=1, source_target_pairs={{0,8},{8,16},{16,24},{24,0},{1,9},{9,17},{17,25},{25,1},{2,10},{10... | collective-permute-start | bytes 737288 | tf_op jit(solution)/shard_map/ppermute | solution.py:327
  103.7 11.5 %all-to-all-start.5 = ((bf16[8,120,128]{2,1,0:T(8,128)(2,1)}), bf16[8,120,128]{2,1,0:T(8,128)(2,1)S(1)}, u32[]{:S(2)}, u32[]{:S(2)}) async-start(bf16[8,120,128]{2,1,0:T(8,128)(2,1)} %shard_map.78), calls=%async_computation.5 | async-start | bytes 491520 | tf_op jit(solution)/shard_map/all_to_all | solution.py:331

commit v4 on v3

--- a/solution.py
+++ b/solution.py
@@ -109,19 +109,19 @@
 def spatial_kernel(height, width, picks, stream, *refs):
     if picks:
         _, entering_ref, *refs = refs
-    passed_ref, weight_ref, out_ref, taps, *refs = refs
+    if stream:
+        passed_ref, weight_ref, later_ref, out_ref, held_ref, taps, kernels, sems = refs
+    else:
+        passed_ref, weight_ref, out_ref, taps = refs
+        kernels = weight_ref
     cells, channels = height * width, weight_ref.shape[-1]
     copies = []
-    kernels = weight_ref
     if stream:
-        kernels, sems = refs
-        for layer in range(2):
-            for row in range(3):
-                copy = pltpu.make_async_copy(
-                    weight_ref.at[layer, row], kernels.at[layer, row], sems.at[layer, row]
-                )
-                copy.start()
-                copies.append(copy)
+        pairs = [(weight_ref.at[layer, row], kernels.at[layer, row]) for layer in range(2) for row in range(3)]
+        pairs.append((later_ref, held_ref))
+        copies = [pltpu.make_async_copy(source, target, sems.at[i]) for i, (source, target) in enumerate(pairs)]
+        for copy in copies:
+            copy.start()
     edge = jnp.zeros((width, 3 * channels), jnp.bfloat16)
     taps[0:width, :] = edge
     taps[width + cells : 2 * width + cells, :] = edge
@@ -158,9 +158,11 @@
     middle = conv(silu(group_norm(start, same_group)), 0).astype(jnp.bfloat16).astype(jnp.float32)
     after = conv(silu(group_norm(middle, same_group)), 1)
     pack(out_ref, start + after)
-
-
-def spatial_part(height, width, devices, passed, weights, plan=None, entering=None, turn=0):
+    if stream:
+        copies[-1].wait()
+
+
+def spatial_part(height, width, devices, passed, weights, plan=None, entering=None, turn=0, later=None):
     cells, channels = height * width, weights.shape[-1]
     chunks = (devices,) + chunk_shape(cells // devices, channels)
     weights = weights.reshape(2, 3, 3 * channels, weights.shape[-1])
@@ -173,16 +175,23 @@
     if plan is not None:
         specs = [pl.BlockSpec((None, cells, channels), lambda i, order: (order[turn], 0, 0))] + specs
         operands = [plan, entering] + operands
+    out_shape = jax.ShapeDtypeStruct(chunks, jnp.bfloat16)
+    out_specs = pl.BlockSpec(chunks, lambda i, *_: (0, 0, 0))
+    if stream:
+        specs.append(pl.BlockSpec(memory_space=pltpu.HBM))
+        operands.append(later)
+        out_shape = [out_shape, jax.ShapeDtypeStruct(later.shape, later.dtype)]
+        out_specs = [out_specs, pl.BlockSpec(memory_space=pltpu.VMEM)]
     return pl.pallas_call(
         functools.partial(spatial_kernel, height, width, plan is not None, stream),
-        out_shape=jax.ShapeDtypeStruct(chunks, jnp.bfloat16),
+        out_shape=out_shape,
         grid_spec=pltpu.PrefetchScalarGridSpec(
             num_scalar_prefetch=0 if plan is None else 1,
             grid=(1,),
             in_specs=specs,
-            out_specs=pl.BlockSpec(chunks, lambda i, *_: (0, 0, 0)),
+            out_specs=out_specs,
             scratch_shapes=[pltpu.VMEM((cells + 2 * width, 3 * channels), jnp.bfloat16)]
-            + ([pltpu.VMEM(weights.shape, jnp.bfloat16), pltpu.SemaphoreType.DMA((2, 3))] if stream else []),
+            + ([pltpu.VMEM(weights.shape, jnp.bfloat16), pltpu.SemaphoreType.DMA((7,))] if stream else []),
         ),
         compiler_params=pltpu.CompilerParams(vmem_limit_bytes=(52 if stream else 24) * MIB),
     )(*operands)
@@ -322,12 +331,12 @@
     outputs = None
     for tick in range(TICKS):
         if tick == 0:
-            after = spatial_part(height, width, devices, current, spatial_weight[0])
+            after, temporal = spatial_part(height, width, devices, current, spatial_weight[0], later=temporal_weight[0])
         else:
-            passed = lax.ppermute(current, "section", ring)
+            passed, outputs = lax.optimization_barrier((lax.ppermute(current, "section", ring), outputs))
             after = spatial_part(height, width, devices, passed, spatial_weight[0], plan, entering, tick - 1)
         gathered = lax.all_to_all(after, "seq", split_axis=0, concat_axis=0, tiled=True)
-        done = temporal_part(devices, share, gathered, temporal_weight[0], attn_in[0], attn_out[0])
+        done = temporal_part(devices, share, gathered, temporal, attn_in[0], attn_out[0])
         current = lax.all_to_all(done, "seq", split_axis=0, concat_axis=0, tiled=True)
         outputs = collect(tick, current, (TICKS, cells, channels), outputs)
     return outputs.reshape(TICKS, 1, 1, height, width, channels)

time: 117 us -> 114 us (0.974)
  blocking collectives: 61.3 us -> 72.1 us
  waiting for transfers between devices: 17.7 us -> 9.61 us
  starting transfers between devices: 3.41 us -> 0.01 us
  local copies, waits for them, and re-layouts: 2.36 us -> 0.98 us
    all_to_all x2 -> x3, blocking collectives: 22.9 us -> 33.6 us  [shards(): lax.all_to_all(done, 'seq', split_axis=0, concat_axis=0, tiled=True)]
    all_to_all x1 -> x0, waiting for transfers between devices: 6.42 us -> none  [shards(): lax.all_to_all(done, 'seq', split_axis=0, concat_axis=0, tiled=True)]
    all_to_all x1 -> x0, starting transfers between devices: 3.41 us -> none  [shards(): lax.all_to_all(done, 'seq', split_axis=0, concat_axis=0, tiled=True)]
    ppermute x2, waiting for transfers between devices: 11.2 us -> 9.61 us  [shards(): lax.ppermute(current, 'section', ring)]
    unnamed x16 -> x12, local copies, waits for them, and re-layouts: 2.36 us -> 0.98 us
  transfers between devices with their start and end apart: 3 -> 2, of which waited for: 3 -> 2; matrix products, arithmetic and copies ran while one was open for 0% -> 0% of each run, Pallas kernels for 1% -> 1%
where the time goes in v4:
time: 114 us; the launch traced here: 113 us
  blocking collectives  72.1 us (63%)
  Pallas kernels  30.6 us (27%)
  waiting for transfers between devices  9.61 us (8%)
    all_to_all x3, blocking collectives, shards(): lax.all_to_all(after, 'seq', split_axis=0, concat_axis=0, tiled=True)  38.4 us
    all_to_all x3, blocking collectives, shards(): lax.all_to_all(done, 'seq', split_axis=0, concat_axis=0, tiled=True)  33.6 us
    pallas_call x3, Pallas kernels, spatial_part(): pl.pallas_call(functools.partial(spatial_kernel, height, width, plan is n...  15.3 us
    pallas_call x3, Pallas kernels, temporal_part(): pl.pallas_call(functools.partial(temporal_kernel, frames, items), out_sha...  12.8 us
    ppermute x2, waiting for transfers between devices, shards(): lax.ppermute(current, 'section', ring)  9.61 us
    pallas_call x3, Pallas kernels, collect(): pl.pallas_call(functools.partial(collect_kernel, tick), out_shape=jax.Sha...  2.42 us
  transfers between devices with their start and end apart: 2, of which 2 were waited for; matrix products, arithmetic and copies ran while one was open for 0% of the time, Pallas kernels for 1%

profile of v4, /device:TPU:0, one launch (start us, length us, event | category | flops | bytes accessed | tf_op | source)
XLA Modules:
  0.0 113.4 jit_solution(5519080269780263803)
XLA Ops:
  0.0 0.0 copy-start.4
  0.0 1.0 copy-done.4
  1.0 0.0 copy-start.1
  1.0 0.0 copy-start.3
  1.0 0.0 copy-start.2
  1.0 5.5 %shard_map.73 = (bf16[8,120,128]{2,1,0:T(8,128)(2,1)S(1)}, bf16[2,3,320,320]{3,2,1,0:T(8,128)(2,1)S(1)}) custom-call(bf16[384,320]{1,0:T(8,128)(2,1)S(1)} %bitcast.24, bf16[2,3,960,320]{3,2,1,0:T(8,128)(2,1)} %bitcast.10, bf16[2,3,320,320]{3,2,1,0:T(8,128)(2,1)} %bitcast.25), custom_call_target="tpu_custom_call" | custom-call | tf_op jit(solution)/shard_map/pallas_call | solution.py:185
  6.5 15.8 %all_to_all.30.in_ref = bf16[8,120,128]{2,1,0:T(8,128)(2,1)S(1)} all-to-all(bf16[8,120,128]{2,1,0:T(8,128)(2,1)S(1)} %get-tuple-element.11), channel_id=1, replica_groups=mesh['section'=4,'seq'=8] {'seq'}, dimensions={0} | all-to-all | bytes 491520 | tf_op jit(solution)/shard_map/all_to_all | solution.py:338
  22.2 0.0 copy-done.1
  22.2 0.0 copy-done.3
  22.2 0.0 copy-start
  22.3 4.3 %shard_map.74 = bf16[8,120,128]{2,1,0:T(8,128)(2,1)S(1)} custom-call(bf16[8,120,128]{2,1,0:T(8,128)(2,1)S(1)} %all_to_all.30.in_ref, bf16[2,960,320]{2,1,0:T(8,128)(2,1)S(1)} %bitcast.13, bf16[320,960]{1,0:T(8,128)(2,1)S(1)} %bitcast.16, bf16[320,320]{1,0:T(8,128)(2,1)S(1)} %bitcast.21), custom_call_target="tpu_custom_call" | custom-call | tf_op jit(solution)/shard_map/pallas_call | solution.py:288
  26.5 0.0 copy-start.5
  26.5 11.6 %all_to_all.31.refs_0_ = bf16[8,120,128]{2,1,0:T(8,128)(2,1)S(1)} all-to-all(bf16[8,120,128]{2,1,0:T(8,128)(2,1)S(1)} %shard_map.74), channel_id=1, replica_groups=mesh['section'=4,'seq'=8] {'seq'}, dimensions={0} | all-to-all | bytes 491520 | tf_op jit(solution)/shard_map/all_to_all | solution.py:340
  38.2 0.0 collective-permute-start
  38.2 0.8 shard_map.75.refs_1_
  39.0 4.8 %collective-permute-done.refs_2_ = bf16[8,120,128]{2,1,0:T(8,128)(2,1)S(1)} collective-permute-done((bf16[8,120,128]{2,1,0:T(8,128)(2,1)S(1)}, bf16[8,120,128]{2,1,0:T(8,128)(2,1)S(1)}, u32[]{:S(2)}, u32[]{:S(2)}) %collective-permute-start) | collective-permute-done | bytes 245792 | tf_op jit(solution)/shard_map/ppermute | solution.py:336
  43.8 0.0 copy-done.2
  43.8 0.0 copy-done
  43.8 0.0 copy-done.5
  43.8 4.9 %shard_map.76 = bf16[8,120,128]{2,1,0:T(8,128)(2,1)S(1)} custom-call(s32[4]{0:T(128)S(1)} %copy-done.5, bf16[4,384,320]{2,1,0:T(8,128)(2,1)S(1)} %bitcast.19, bf16[8,120,128]{2,1,0:T(8,128)(2,1)S(1)} %collective-permute-done.refs_2_, bf16[2,3,960,320]{3,2,1,0:T(8,128)(2,1)S(1)} %bitcast.11), custom_call_target="tpu_custom_call" | custom-call | tf_op jit(solution)/shard_map/pallas_call | solution.py:185
  48.7 11.4 %all_to_all.32.in_ref = bf16[8,120,128]{2,1,0:T(8,128)(2,1)S(1)} all-to-all(bf16[8,120,128]{2,1,0:T(8,128)(2,1)S(1)} %shard_map.76), channel_id=1, replica_groups=mesh['section'=4,'seq'=8] {'seq'}, dimensions={0} | all-to-all | bytes 491520 | tf_op jit(solution)/shard_map/all_to_all | solution.py:338
  60.1 4.3 %shard_map.77 = bf16[8,120,128]{2,1,0:T(8,128)(2,1)S(1)} custom-call(bf16[8,120,128]{2,1,0:T(8,128)(2,1)S(1)} %all_to_all.32.in_ref, bf16[2,960,320]{2,1,0:T(8,128)(2,1)S(1)} %bitcast.14, bf16[320,960]{1,0:T(8,128)(2,1)S(1)} %bitcast.17, bf16[320,320]{1,0:T(8,128)(2,1)S(1)} %bitcast.22), custom_call_target="tpu_custom_call" | custom-call | tf_op jit(solution)/shard_map/pallas_call | solution.py:288
  64.4 11.3 %all_to_all.33.refs_0_ = bf16[8,120,128]{2,1,0:T(8,128)(2,1)S(1)} all-to-all(bf16[8,120,128]{2,1,0:T(8,128)(2,1)S(1)} %shard_map.77), channel_id=1, replica_groups=mesh['section'=4,'seq'=8] {'seq'}, dimensions={0} | all-to-all | bytes 491520 | tf_op jit(solution)/shard_map/all_to_all | solution.py:340
  75.6 0.0 collective-permute-start.1
  75.6 0.8 shard_map.78.refs_1_
  76.5 4.8 %collective-permute-done.1.refs_2_ = bf16[8,120,128]{2,1,0:T(8,128)(2,1)S(1)} collective-permute-done((bf16[8,120,128]{2,1,0:T(8,128)(2,1)S(1)}, bf16[8,120,128]{2,1,0:T(8,128)(2,1)S(1)}, u32[]{:S(2)}, u32[]{:S(2)}) %collective-permute-start.1) | collective-permute-done | bytes 245792 | tf_op jit(solution)/shard_map/ppermute | solution.py:336
  81.3 4.9 %shard_map.79 = bf16[8,120,128]{2,1,0:T(8,128)(2,1)S(1)} custom-call(s32[4]{0:T(128)S(1)} %copy-done.5, bf16[4,384,320]{2,1,0:T(8,128)(2,1)S(1)} %bitcast.20, bf16[8,120,128]{2,1,0:T(8,128)(2,1)S(1)} %collective-permute-done.1.refs_2_, bf16[2,3,960,320]{3,2,1,0:T(8,128)(2,1)S(1)} %bitcast.12), custom_call_target="tpu_custom_call" | custom-call | tf_op jit(solution)/shard_map/pallas_call | solution.py:185
  86.2 11.3 %all_to_all.34.in_ref = bf16[8,120,128]{2,1,0:T(8,128)(2,1)S(1)} all-to-all(bf16[8,120,128]{2,1,0:T(8,128)(2,1)S(1)} %shard_map.79), channel_id=1, replica_groups=mesh['section'=4,'seq'=8] {'seq'}, dimensions={0} | all-to-all | bytes 491520 | tf_op jit(solution)/shard_map/all_to_all | solution.py:338
  97.5 4.3 %shard_map.80 = bf16[8,120,128]{2,1,0:T(8,128)(2,1)S(1)} custom-call(bf16[8,120,128]{2,1,0:T(8,128)(2,1)S(1)} %all_to_all.34.in_ref, bf16[2,960,320]{2,1,0:T(8,128)(2,1)S(1)} %bitcast.15, bf16[320,960]{1,0:T(8,128)(2,1)S(1)} %bitcast.18, bf16[320,320]{1,0:T(8,128)(2,1)S(1)} %bitcast.23), custom_call_target="tpu_custom_call" | custom-call | tf_op jit(solution)/shard_map/pallas_call | solution.py:288
  101.7 10.7 %all_to_all.35.refs_0_ = bf16[8,120,128]{2,1,0:T(8,128)(2,1)S(1)} all-to-all(bf16[8,120,128]{2,1,0:T(8,128)(2,1)S(1)} %shard_map.80), channel_id=1, replica_groups=mesh['section'=4,'seq'=8] {'seq'}, dimensions={0} | all-to-all | bytes 491520 | tf_op jit(solution)/shard_map/all_to_all | solution.py:340
  112.5 0.8 shard_map.81
Async XLA Ops:
  0.0 1.0 copy-start.4
  1.0 21.3 %copy-start.1 = (bf16[1,320,960]{2,1,0:T(8,128)(2,1)S(1)}, bf16[1,320,960]{2,1,0:T(8,128)(2,1)}, u32[]{:S(2)}) copy-start(bf16[1,320,960]{2,1,0:T(8,128)(2,1)} %param.12) | copy-start | bytes 1843204
  1.0 21.3 %copy-start.3 = (bf16[1,320,320]{2,1,0:T(8,128)(2,1)S(1)}, bf16[1,320,320]{2,1,0:T(8,128)(2,1)}, u32[]{:S(2)}) copy-start(bf16[1,320,320]{2,1,0:T(8,128)(2,1)} %param.13) | copy-start | bytes 614404
  1.0 42.8 %copy-start.2 = (bf16[4,1,16,24,320]{4,3,2,1,0:T(8,128)(2,1)S(1)}, bf16[4,1,16,24,320]{4,3,2,1,0:T(8,128)(2,1)}, u32[]{:S(2)}) copy-start(bf16[4,1,16,24,320]{4,3,2,1,0:T(8,128)(2,1)} %param.7) | copy-start | bytes 2949124
  22.2 21.5 %copy-start = (bf16[1,2,9,320,320]{4,3,2,1,0:T(8,128)(2,1)S(1)}, bf16[1,2,9,320,320]{4,3,2,1,0:T(8,128)(2,1)}, u32[]{:S(2)}) copy-start(bf16[1,2,9,320,320]{4,3,2,1,0:T(8,128)(2,1)} %param.10) | copy-start | bytes 11059204
  26.5 17.3 %copy-start.5 = (s32[4]{0:T(128)S(1)}, s32[4]{0:T(128)}, u32[]{:S(2)}) copy-start(s32[4]{0:T(128)} %refs_0_.3) | copy-start | bytes 52
  38.2 5.6 %collective-permute-start = (bf16[8,120,128]{2,1,0:T(8,128)(2,1)S(1)}, bf16[8,120,128]{2,1,0:T(8,128)(2,1)S(1)}, u32[]{:S(2)}, u32[]{:S(2)}) collective-permute-start(bf16[8,120,128]{2,1,0:T(8,128)(2,1)S(1)} %all_to_all.31.refs_0_), channel_id=1, source_target_pairs={{0,8},{8,16},{16,24},{24,0},{1,9},{9,17},{17,25},{25,1},{2,10},{10... | collective-permute-start | bytes 737288 | tf_op jit(solution)/shard_map/ppermute | solution.py:336
  75.6 5.6 %collective-permute-start.1 = (bf16[8,120,128]{2,1,0:T(8,128)(2,1)S(1)}, bf16[8,120,128]{2,1,0:T(8,128)(2,1)S(1)}, u32[]{:S(2)}, u32[]{:S(2)}) collective-permute-start(bf16[8,120,128]{2,1,0:T(8,128)(2,1)S(1)} %all_to_all.33.refs_0_), channel_id=1, source_target_pairs={{0,8},{8,16},{16,24},{24,0},{1,9},{9,17},{17,25},{25,1},{2,10},{10... | collective-permute-start | bytes 737288 | tf_op jit(solution)/shard_map/ppermute | solution.py:336

commit v5 on v4

--- a/solution.py
+++ b/solution.py
@@ -85,10 +85,13 @@
 def group_norm(values, same_group):
     cells, channels = values.shape
     scale = 1.0 / (cells * (channels // GROUPS))
-    center = group_total(jnp.sum(values.reshape(-1, 8, channels), axis=0), same_group) * scale
-    shifted = values - center
-    spread = group_total(jnp.sum(jnp.square(shifted).reshape(-1, 8, channels), axis=0), same_group) * scale
-    return shifted * lax.rsqrt(spread + EPSILON)
+    partial = jnp.sum(values.reshape(-1, 8, channels), axis=0)
+    center = group_total(partial, same_group) * scale
+    own = jnp.sum(partial, axis=0, keepdims=True) * (1.0 / cells)
+    squares = jnp.sum(jnp.square(values - own).reshape(-1, 8, channels), axis=0)
+    squares = squares + jnp.square(own - center) * (cells / 8)
+    spread = group_total(squares, same_group) * scale
+    return (values - center) * lax.rsqrt(spread + EPSILON)
 
 
 def layer_norm(values, ones):
@@ -138,17 +141,11 @@
         taps[width : width + cells, 0:channels] = left.astype(jnp.bfloat16)
         taps[width : width + cells, channels : 2 * channels] = values.astype(jnp.bfloat16)
         taps[width : width + cells, 2 * channels : 3 * channels] = right.astype(jnp.bfloat16)
-        total = None
-        for row in range(3):
-            if stream:
+        if stream:
+            for row in range(3):
                 copies[3 * layer + row].wait()
-            part = jnp.dot(
-                taps[row * width : row * width + cells, :],
-                kernels[layer, row],
-                preferred_element_type=jnp.float32,
-            )
-            total = part if total is None else total + part
-        return total
+        lhs = jnp.concatenate([taps[row * width : row * width + cells, :] for row in range(3)], axis=1)
+        return jnp.dot(lhs, kernels[layer].reshape(9 * channels, channels), preferred_element_type=jnp.float32)
 
     if picks:
         entering = entering_ref[...].astype(jnp.float32)
@@ -259,12 +256,12 @@
                     [jnp.where(owner == head, chosen, jnp.zeros_like(chosen)) for head in range(heads)], axis=0
                 )
             scores = lax.dot_general(
-                chosen, k[:, low:high], (((1,), (1,)), ((), ())), preferred_element_type=jnp.float32
+                k[:, low:high], chosen, (((1,), (1,)), ((), ())), preferred_element_type=jnp.float32
             )
-            scores = scores.reshape(heads, size, size) * scale + blocked
-            top = jnp.max(scores, axis=-1, keepdims=True)
-            raised = jnp.exp2(scores - top).astype(jnp.bfloat16).reshape(heads * size, size)
-            both = jnp.dot(raised, jnp.concatenate([tall, v[:, low:high]], axis=1), preferred_element_type=jnp.float32)
+            scores = scores * scale + jnp.concatenate([blocked] * heads, axis=1)
+            top = jnp.max(scores, axis=0, keepdims=True)
+            raised = jnp.exp2(scores - top).astype(jnp.bfloat16)
+            both = lax.dot_general(raised, jnp.concatenate([tall, v[:, low:high]], axis=1), (((0,), (0,)), ((), ())), preferred_element_type=jnp.float32)
             share = both[:, LANES:] / both[:, : high - low]
             out = share[0:size]
             for head in range(1, heads):

time: 114 us -> 113 us (level)
  no operation moved by 1% of the time
where the time goes in v5:
time: 113 us
  blocking collectives  72.1 us (64%)
  Pallas kernels  29.6 us (26%)
  waiting for transfers between devices  9.61 us (9%)
    all_to_all x3, blocking collectives, shards(): lax.all_to_all(after, 'seq', split_axis=0, concat_axis=0, tiled=True)  38.5 us
    all_to_all x3, blocking collectives, shards(): lax.all_to_all(done, 'seq', split_axis=0, concat_axis=0, tiled=True)  33.6 us
    pallas_call x3, Pallas kernels, spatial_part(): pl.pallas_call(functools.partial(spatial_kernel, height, width, plan is n...  14.6 us
    pallas_call x3, Pallas kernels, temporal_part(): pl.pallas_call(functools.partial(temporal_kernel, frames, items), out_sha...  12.6 us
    ppermute x2, waiting for transfers between devices, shards(): lax.ppermute(current, 'section', ring)  9.61 us
    pallas_call x3, Pallas kernels, collect(): pl.pallas_call(functools.partial(collect_kernel, tick), out_shape=jax.Sha...  2.42 us
  transfers between devices with their start and end apart: 2, of which 2 were waited for; matrix products, arithmetic and copies ran while one was open for 0% of the time, Pallas kernels for 1%

profile of v5, /device:TPU:0, one launch (start us, length us, event | category | flops | bytes accessed | tf_op | source)
XLA Modules:
  0.0 112.5 jit_solution(8389259747724493469)
XLA Ops:
  0.0 0.0 copy-start.4
  0.0 1.0 copy-done.4
  1.0 0.0 copy-start.1
  1.0 0.0 copy-start.3
  1.0 0.0 copy-start.2
  1.0 5.3 %shard_map.73 = (bf16[8,120,128]{2,1,0:T(8,128)(2,1)S(1)}, bf16[2,3,320,320]{3,2,1,0:T(8,128)(2,1)S(1)}) custom-call(bf16[384,320]{1,0:T(8,128)(2,1)S(1)} %bitcast.24, bf16[2,3,960,320]{3,2,1,0:T(8,128)(2,1)} %bitcast.10, bf16[2,3,320,320]{3,2,1,0:T(8,128)(2,1)} %bitcast.25), custom_call_target="tpu_custom_call" | custom-call | tf_op jit(solution)/shard_map/pallas_call | solution.py:182
  6.3 15.8 %all_to_all.30.in_ref = bf16[8,120,128]{2,1,0:T(8,128)(2,1)S(1)} all-to-all(bf16[8,120,128]{2,1,0:T(8,128)(2,1)S(1)} %get-tuple-element.11), channel_id=1, replica_groups=mesh['section'=4,'seq'=8] {'seq'}, dimensions={0} | all-to-all | bytes 491520 | tf_op jit(solution)/shard_map/all_to_all | solution.py:335
  22.0 0.0 copy-done.1
  22.0 0.0 copy-done.3
  22.0 0.0 copy-start
  22.0 4.2 %shard_map.74 = bf16[8,120,128]{2,1,0:T(8,128)(2,1)S(1)} custom-call(bf16[8,120,128]{2,1,0:T(8,128)(2,1)S(1)} %all_to_all.30.in_ref, bf16[2,960,320]{2,1,0:T(8,128)(2,1)S(1)} %bitcast.13, bf16[320,960]{1,0:T(8,128)(2,1)S(1)} %bitcast.16, bf16[320,320]{1,0:T(8,128)(2,1)S(1)} %bitcast.21), custom_call_target="tpu_custom_call" | custom-call | tf_op jit(solution)/shard_map/pallas_call | solution.py:285
  26.2 0.0 copy-start.5
  26.3 11.6 %all_to_all.31.refs_0_ = bf16[8,120,128]{2,1,0:T(8,128)(2,1)S(1)} all-to-all(bf16[8,120,128]{2,1,0:T(8,128)(2,1)S(1)} %shard_map.74), channel_id=1, replica_groups=mesh['section'=4,'seq'=8] {'seq'}, dimensions={0} | all-to-all | bytes 491520 | tf_op jit(solution)/shard_map/all_to_all | solution.py:337
  37.9 0.0 collective-permute-start
  37.9 0.8 shard_map.75.refs_1_
  38.7 4.8 %collective-permute-done.refs_2_ = bf16[8,120,128]{2,1,0:T(8,128)(2,1)S(1)} collective-permute-done((bf16[8,120,128]{2,1,0:T(8,128)(2,1)S(1)}, bf16[8,120,128]{2,1,0:T(8,128)(2,1)S(1)}, u32[]{:S(2)}, u32[]{:S(2)}) %collective-permute-start) | collective-permute-done | bytes 245792 | tf_op jit(solution)/shard_map/ppermute | solution.py:333
  43.5 0.0 copy-done.2
  43.5 0.0 copy-done
  43.5 0.0 copy-done.5
  43.5 4.6 %shard_map.76 = bf16[8,120,128]{2,1,0:T(8,128)(2,1)S(1)} custom-call(s32[4]{0:T(128)S(1)} %copy-done.5, bf16[4,384,320]{2,1,0:T(8,128)(2,1)S(1)} %bitcast.19, bf16[8,120,128]{2,1,0:T(8,128)(2,1)S(1)} %collective-permute-done.refs_2_, bf16[2,3,960,320]{3,2,1,0:T(8,128)(2,1)S(1)} %bitcast.11), custom_call_target="tpu_custom_call" | custom-call | tf_op jit(solution)/shard_map/pallas_call | solution.py:182
  48.2 11.4 %all_to_all.32.in_ref = bf16[8,120,128]{2,1,0:T(8,128)(2,1)S(1)} all-to-all(bf16[8,120,128]{2,1,0:T(8,128)(2,1)S(1)} %shard_map.76), channel_id=1, replica_groups=mesh['section'=4,'seq'=8] {'seq'}, dimensions={0} | all-to-all | bytes 491520 | tf_op jit(solution)/shard_map/all_to_all | solution.py:335
  59.6 4.2 %shard_map.77 = bf16[8,120,128]{2,1,0:T(8,128)(2,1)S(1)} custom-call(bf16[8,120,128]{2,1,0:T(8,128)(2,1)S(1)} %all_to_all.32.in_ref, bf16[2,960,320]{2,1,0:T(8,128)(2,1)S(1)} %bitcast.14, bf16[320,960]{1,0:T(8,128)(2,1)S(1)} %bitcast.17, bf16[320,320]{1,0:T(8,128)(2,1)S(1)} %bitcast.22), custom_call_target="tpu_custom_call" | custom-call | tf_op jit(solution)/shard_map/pallas_call | solution.py:285
  63.8 11.3 %all_to_all.33.refs_0_ = bf16[8,120,128]{2,1,0:T(8,128)(2,1)S(1)} all-to-all(bf16[8,120,128]{2,1,0:T(8,128)(2,1)S(1)} %shard_map.77), channel_id=1, replica_groups=mesh['section'=4,'seq'=8] {'seq'}, dimensions={0} | all-to-all | bytes 491520 | tf_op jit(solution)/shard_map/all_to_all | solution.py:337
  75.0 0.0 collective-permute-start.1
  75.0 0.8 shard_map.78.refs_1_
  75.8 4.8 %collective-permute-done.1.refs_2_ = bf16[8,120,128]{2,1,0:T(8,128)(2,1)S(1)} collective-permute-done((bf16[8,120,128]{2,1,0:T(8,128)(2,1)S(1)}, bf16[8,120,128]{2,1,0:T(8,128)(2,1)S(1)}, u32[]{:S(2)}, u32[]{:S(2)}) %collective-permute-start.1) | collective-permute-done | bytes 245792 | tf_op jit(solution)/shard_map/ppermute | solution.py:333
  80.7 4.6 %shard_map.79 = bf16[8,120,128]{2,1,0:T(8,128)(2,1)S(1)} custom-call(s32[4]{0:T(128)S(1)} %copy-done.5, bf16[4,384,320]{2,1,0:T(8,128)(2,1)S(1)} %bitcast.20, bf16[8,120,128]{2,1,0:T(8,128)(2,1)S(1)} %collective-permute-done.1.refs_2_, bf16[2,3,960,320]{3,2,1,0:T(8,128)(2,1)S(1)} %bitcast.12), custom_call_target="tpu_custom_call" | custom-call | tf_op jit(solution)/shard_map/pallas_call | solution.py:182
  85.3 11.3 %all_to_all.34.in_ref = bf16[8,120,128]{2,1,0:T(8,128)(2,1)S(1)} all-to-all(bf16[8,120,128]{2,1,0:T(8,128)(2,1)S(1)} %shard_map.79), channel_id=1, replica_groups=mesh['section'=4,'seq'=8] {'seq'}, dimensions={0} | all-to-all | bytes 491520 | tf_op jit(solution)/shard_map/all_to_all | solution.py:335
  96.6 4.2 %shard_map.80 = bf16[8,120,128]{2,1,0:T(8,128)(2,1)S(1)} custom-call(bf16[8,120,128]{2,1,0:T(8,128)(2,1)S(1)} %all_to_all.34.in_ref, bf16[2,960,320]{2,1,0:T(8,128)(2,1)S(1)} %bitcast.15, bf16[320,960]{1,0:T(8,128)(2,1)S(1)} %bitcast.18, bf16[320,320]{1,0:T(8,128)(2,1)S(1)} %bitcast.23), custom_call_target="tpu_custom_call" | custom-call | tf_op jit(solution)/shard_map/pallas_call | solution.py:285
  100.8 10.7 %all_to_all.35.refs_0_ = bf16[8,120,128]{2,1,0:T(8,128)(2,1)S(1)} all-to-all(bf16[8,120,128]{2,1,0:T(8,128)(2,1)S(1)} %shard_map.80), channel_id=1, replica_groups=mesh['section'=4,'seq'=8] {'seq'}, dimensions={0} | all-to-all | bytes 491520 | tf_op jit(solution)/shard_map/all_to_all | solution.py:337
  111.5 0.8 shard_map.81
Async XLA Ops:
  0.0 1.0 copy-start.4
  1.0 21.1 %copy-start.1 = (bf16[1,320,960]{2,1,0:T(8,128)(2,1)S(1)}, bf16[1,320,960]{2,1,0:T(8,128)(2,1)}, u32[]{:S(2)}) copy-start(bf16[1,320,960]{2,1,0:T(8,128)(2,1)} %param.12) | copy-start | bytes 1843204
  1.0 21.1 %copy-start.3 = (bf16[1,320,320]{2,1,0:T(8,128)(2,1)S(1)}, bf16[1,320,320]{2,1,0:T(8,128)(2,1)}, u32[]{:S(2)}) copy-start(bf16[1,320,320]{2,1,0:T(8,128)(2,1)} %param.13) | copy-start | bytes 614404
  1.0 42.5 %copy-start.2 = (bf16[4,1,16,24,320]{4,3,2,1,0:T(8,128)(2,1)S(1)}, bf16[4,1,16,24,320]{4,3,2,1,0:T(8,128)(2,1)}, u32[]{:S(2)}) copy-start(bf16[4,1,16,24,320]{4,3,2,1,0:T(8,128)(2,1)} %param.7) | copy-start | bytes 2949124
  22.0 21.5 %copy-start = (bf16[1,2,9,320,320]{4,3,2,1,0:T(8,128)(2,1)S(1)}, bf16[1,2,9,320,320]{4,3,2,1,0:T(8,128)(2,1)}, u32[]{:S(2)}) copy-start(bf16[1,2,9,320,320]{4,3,2,1,0:T(8,128)(2,1)} %param.10) | copy-start | bytes 11059204
  26.2 17.3 %copy-start.5 = (s32[4]{0:T(128)S(1)}, s32[4]{0:T(128)}, u32[]{:S(2)}) copy-start(s32[4]{0:T(128)} %refs_0_.3) | copy-start | bytes 52
  37.9 5.6 %collective-permute-start = (bf16[8,120,128]{2,1,0:T(8,128)(2,1)S(1)}, bf16[8,120,128]{2,1,0:T(8,128)(2,1)S(1)}, u32[]{:S(2)}, u32[]{:S(2)}) collective-permute-start(bf16[8,120,128]{2,1,0:T(8,128)(2,1)S(1)} %all_to_all.31.refs_0_), channel_id=1, source_target_pairs={{0,8},{8,16},{16,24},{24,0},{1,9},{9,17},{17,25},{25,1},{2,10},{10... | collective-permute-start | bytes 737288 | tf_op jit(solution)/shard_map/ppermute | solution.py:333
  75.0 5.6 %collective-permute-start.1 = (bf16[8,120,128]{2,1,0:T(8,128)(2,1)S(1)}, bf16[8,120,128]{2,1,0:T(8,128)(2,1)S(1)}, u32[]{:S(2)}, u32[]{:S(2)}) collective-permute-start(bf16[8,120,128]{2,1,0:T(8,128)(2,1)S(1)} %all_to_all.33.refs_0_), channel_id=1, source_target_pairs={{0,8},{8,16},{16,24},{24,0},{1,9},{9,17},{17,25},{25,1},{2,10},{10... | collective-permute-start | bytes 737288 | tf_op jit(solution)/shard_map/ppermute | solution.py:333

commit v6 on v5

--- a/solution.py
+++ b/solution.py
@@ -202,11 +202,10 @@
         if aligned:
             whole = values.astype(jnp.bfloat16)
             edge = jnp.zeros((items, channels), jnp.bfloat16)
-            taps[0:items, 0:channels] = edge
-            taps[items:rows, 0:channels] = whole[0 : rows - items]
-            taps[:, channels : 2 * channels] = whole
-            taps[0 : rows - items, 2 * channels : 3 * channels] = whole[items:rows]
-            taps[rows - items : rows, 2 * channels : 3 * channels] = edge
+            before = jnp.concatenate([edge, whole[0 : rows - items]], axis=0)
+            behind = jnp.concatenate([whole[items:rows], edge], axis=0)
+            lhs = jnp.concatenate([before, whole, behind], axis=1)
+            return jnp.dot(lhs, kernels[layer], preferred_element_type=jnp.float32)
         else:
             row = lax.broadcasted_iota(jnp.int32, (rows, channels), 0)
             before = jnp.where(row < items, 0.0, pltpu.roll(values, items, 0))
@@ -222,10 +221,8 @@
     after = (start + conv(silu(layer_norm(middle, ones)), 1)).astype(jnp.bfloat16)
 
     normed = layer_norm(after, ones).astype(jnp.bfloat16)
-    taps[...] = jnp.dot(normed, packed[...], preferred_element_type=jnp.float32).astype(jnp.bfloat16)
-    queries = taps[:, 0:channels]
-    keys = taps[:, channels : 2 * channels]
-    values = taps[:, 2 * channels : 3 * channels]
+    projected = jnp.dot(normed, packed[...], preferred_element_type=jnp.float32).astype(jnp.bfloat16)
+    queries, keys, values = [projected[:, i * channels : (i + 1) * channels] for i in range(3)]
 
     head_size = channels // HEADS
     block = 16 if aligned else items

time: 113 us -> 113 us (level)
  no operation moved by 1% of the time
where the time goes in v6:
time: 113 us; the launch traced here: 112 us
  blocking collectives  72.1 us (64%)
  Pallas kernels  29.5 us (26%)
  waiting for transfers between devices  9.61 us (9%)
    all_to_all x3, blocking collectives, shards(): lax.all_to_all(after, 'seq', split_axis=0, concat_axis=0, tiled=True)  38.5 us
    all_to_all x3, blocking collectives, shards(): lax.all_to_all(done, 'seq', split_axis=0, concat_axis=0, tiled=True)  33.6 us
    pallas_call x3, Pallas kernels, spatial_part(): pl.pallas_call(functools.partial(spatial_kernel, height, width, plan is n...  14.6 us
    pallas_call x3, Pallas kernels, temporal_part(): pl.pallas_call(functools.partial(temporal_kernel, frames, items), out_sha...  12.5 us
    ppermute x2, waiting for transfers between devices, shards(): lax.ppermute(current, 'section', ring)  9.61 us
    pallas_call x3, Pallas kernels, collect(): pl.pallas_call(functools.partial(collect_kernel, tick), out_shape=jax.Sha...  2.42 us
  transfers between devices with their start and end apart: 2, of which 2 were waited for; matrix products, arithmetic and copies ran while one was open for 0% of the time, Pallas kernels for 1%

profile of v6, /device:TPU:0, one launch (start us, length us, event | category | flops | bytes accessed | tf_op | source)
XLA Modules:
  0.0 112.4 jit_solution(309014303395391719)
XLA Ops:
  0.0 0.0 copy-start.4
  0.0 1.0 copy-done.4
  1.0 0.0 copy-start.1
  1.0 0.0 copy-start.3
  1.0 0.0 copy-start.2
  1.0 5.3 %shard_map.73 = (bf16[8,120,128]{2,1,0:T(8,128)(2,1)S(1)}, bf16[2,3,320,320]{3,2,1,0:T(8,128)(2,1)S(1)}) custom-call(bf16[384,320]{1,0:T(8,128)(2,1)S(1)} %bitcast.24, bf16[2,3,960,320]{3,2,1,0:T(8,128)(2,1)} %bitcast.10, bf16[2,3,320,320]{3,2,1,0:T(8,128)(2,1)} %bitcast.25), custom_call_target="tpu_custom_call" | custom-call | tf_op jit(solution)/shard_map/pallas_call | solution.py:182
  6.3 15.8 %all_to_all.30.in_ref = bf16[8,120,128]{2,1,0:T(8,128)(2,1)S(1)} all-to-all(bf16[8,120,128]{2,1,0:T(8,128)(2,1)S(1)} %get-tuple-element.11), channel_id=1, replica_groups=mesh['section'=4,'seq'=8] {'seq'}, dimensions={0} | all-to-all | bytes 491520 | tf_op jit(solution)/shard_map/all_to_all | solution.py:332
  22.0 0.0 copy-done.1
  22.0 0.0 copy-done.3
  22.0 0.0 copy-start
  22.0 4.2 %shard_map.74 = bf16[8,120,128]{2,1,0:T(8,128)(2,1)S(1)} custom-call(bf16[8,120,128]{2,1,0:T(8,128)(2,1)S(1)} %all_to_all.30.in_ref, bf16[2,960,320]{2,1,0:T(8,128)(2,1)S(1)} %bitcast.13, bf16[320,960]{1,0:T(8,128)(2,1)S(1)} %bitcast.16, bf16[320,320]{1,0:T(8,128)(2,1)S(1)} %bitcast.21), custom_call_target="tpu_custom_call" | custom-call | tf_op jit(solution)/shard_map/pallas_call | solution.py:282
  26.2 0.0 copy-start.5
  26.2 11.6 %all_to_all.31.refs_0_ = bf16[8,120,128]{2,1,0:T(8,128)(2,1)S(1)} all-to-all(bf16[8,120,128]{2,1,0:T(8,128)(2,1)S(1)} %shard_map.74), channel_id=1, replica_groups=mesh['section'=4,'seq'=8] {'seq'}, dimensions={0} | all-to-all | bytes 491520 | tf_op jit(solution)/shard_map/all_to_all | solution.py:334
  37.8 0.0 collective-permute-start
  37.8 0.8 shard_map.75.refs_1_
  38.7 4.8 %collective-permute-done.refs_2_ = bf16[8,120,128]{2,1,0:T(8,128)(2,1)S(1)} collective-permute-done((bf16[8,120,128]{2,1,0:T(8,128)(2,1)S(1)}, bf16[8,120,128]{2,1,0:T(8,128)(2,1)S(1)}, u32[]{:S(2)}, u32[]{:S(2)}) %collective-permute-start) | collective-permute-done | bytes 245792 | tf_op jit(solution)/shard_map/ppermute | solution.py:330
  43.5 0.0 copy-done.2
  43.5 0.0 copy-done
  43.5 0.0 copy-done.5
  43.5 4.6 %shard_map.76 = bf16[8,120,128]{2,1,0:T(8,128)(2,1)S(1)} custom-call(s32[4]{0:T(128)S(1)} %copy-done.5, bf16[4,384,320]{2,1,0:T(8,128)(2,1)S(1)} %bitcast.19, bf16[8,120,128]{2,1,0:T(8,128)(2,1)S(1)} %collective-permute-done.refs_2_, bf16[2,3,960,320]{3,2,1,0:T(8,128)(2,1)S(1)} %bitcast.11), custom_call_target="tpu_custom_call" | custom-call | tf_op jit(solution)/shard_map/pallas_call | solution.py:182
  48.1 11.4 %all_to_all.32.in_ref = bf16[8,120,128]{2,1,0:T(8,128)(2,1)S(1)} all-to-all(bf16[8,120,128]{2,1,0:T(8,128)(2,1)S(1)} %shard_map.76), channel_id=1, replica_groups=mesh['section'=4,'seq'=8] {'seq'}, dimensions={0} | all-to-all | bytes 491520 | tf_op jit(solution)/shard_map/all_to_all | solution.py:332
  59.5 4.2 %shard_map.77 = bf16[8,120,128]{2,1,0:T(8,128)(2,1)S(1)} custom-call(bf16[8,120,128]{2,1,0:T(8,128)(2,1)S(1)} %all_to_all.32.in_ref, bf16[2,960,320]{2,1,0:T(8,128)(2,1)S(1)} %bitcast.14, bf16[320,960]{1,0:T(8,128)(2,1)S(1)} %bitcast.17, bf16[320,320]{1,0:T(8,128)(2,1)S(1)} %bitcast.22), custom_call_target="tpu_custom_call" | custom-call | tf_op jit(solution)/shard_map/pallas_call | solution.py:282
  63.7 11.3 %all_to_all.33.refs_0_ = bf16[8,120,128]{2,1,0:T(8,128)(2,1)S(1)} all-to-all(bf16[8,120,128]{2,1,0:T(8,128)(2,1)S(1)} %shard_map.77), channel_id=1, replica_groups=mesh['section'=4,'seq'=8] {'seq'}, dimensions={0} | all-to-all | bytes 491520 | tf_op jit(solution)/shard_map/all_to_all | solution.py:334
  74.9 0.0 collective-permute-start.1
  75.0 0.8 shard_map.78.refs_1_
  75.8 4.8 %collective-permute-done.1.refs_2_ = bf16[8,120,128]{2,1,0:T(8,128)(2,1)S(1)} collective-permute-done((bf16[8,120,128]{2,1,0:T(8,128)(2,1)S(1)}, bf16[8,120,128]{2,1,0:T(8,128)(2,1)S(1)}, u32[]{:S(2)}, u32[]{:S(2)}) %collective-permute-start.1) | collective-permute-done | bytes 245792 | tf_op jit(solution)/shard_map/ppermute | solution.py:330
  80.6 4.6 %shard_map.79 = bf16[8,120,128]{2,1,0:T(8,128)(2,1)S(1)} custom-call(s32[4]{0:T(128)S(1)} %copy-done.5, bf16[4,384,320]{2,1,0:T(8,128)(2,1)S(1)} %bitcast.20, bf16[8,120,128]{2,1,0:T(8,128)(2,1)S(1)} %collective-permute-done.1.refs_2_, bf16[2,3,960,320]{3,2,1,0:T(8,128)(2,1)S(1)} %bitcast.12), custom_call_target="tpu_custom_call" | custom-call | tf_op jit(solution)/shard_map/pallas_call | solution.py:182
  85.2 11.3 %all_to_all.34.in_ref = bf16[8,120,128]{2,1,0:T(8,128)(2,1)S(1)} all-to-all(bf16[8,120,128]{2,1,0:T(8,128)(2,1)S(1)} %shard_map.79), channel_id=1, replica_groups=mesh['section'=4,'seq'=8] {'seq'}, dimensions={0} | all-to-all | bytes 491520 | tf_op jit(solution)/shard_map/all_to_all | solution.py:332
  96.5 4.2 %shard_map.80 = bf16[8,120,128]{2,1,0:T(8,128)(2,1)S(1)} custom-call(bf16[8,120,128]{2,1,0:T(8,128)(2,1)S(1)} %all_to_all.34.in_ref, bf16[2,960,320]{2,1,0:T(8,128)(2,1)S(1)} %bitcast.15, bf16[320,960]{1,0:T(8,128)(2,1)S(1)} %bitcast.18, bf16[320,320]{1,0:T(8,128)(2,1)S(1)} %bitcast.23), custom_call_target="tpu_custom_call" | custom-call | tf_op jit(solution)/shard_map/pallas_call | solution.py:282
  100.7 10.7 %all_to_all.35.refs_0_ = bf16[8,120,128]{2,1,0:T(8,128)(2,1)S(1)} all-to-all(bf16[8,120,128]{2,1,0:T(8,128)(2,1)S(1)} %shard_map.80), channel_id=1, replica_groups=mesh['section'=4,'seq'=8] {'seq'}, dimensions={0} | all-to-all | bytes 491520 | tf_op jit(solution)/shard_map/all_to_all | solution.py:334
  111.4 0.8 shard_map.81
Async XLA Ops:
  0.0 1.0 copy-start.4
  1.0 21.1 %copy-start.1 = (bf16[1,320,960]{2,1,0:T(8,128)(2,1)S(1)}, bf16[1,320,960]{2,1,0:T(8,128)(2,1)}, u32[]{:S(2)}) copy-start(bf16[1,320,960]{2,1,0:T(8,128)(2,1)} %param.12) | copy-start | bytes 1843204
  1.0 21.1 %copy-start.3 = (bf16[1,320,320]{2,1,0:T(8,128)(2,1)S(1)}, bf16[1,320,320]{2,1,0:T(8,128)(2,1)}, u32[]{:S(2)}) copy-start(bf16[1,320,320]{2,1,0:T(8,128)(2,1)} %param.13) | copy-start | bytes 614404
  1.0 42.5 %copy-start.2 = (bf16[4,1,16,24,320]{4,3,2,1,0:T(8,128)(2,1)S(1)}, bf16[4,1,16,24,320]{4,3,2,1,0:T(8,128)(2,1)}, u32[]{:S(2)}) copy-start(bf16[4,1,16,24,320]{4,3,2,1,0:T(8,128)(2,1)} %param.7) | copy-start | bytes 2949124
  22.0 21.4 %copy-start = (bf16[1,2,9,320,320]{4,3,2,1,0:T(8,128)(2,1)S(1)}, bf16[1,2,9,320,320]{4,3,2,1,0:T(8,128)(2,1)}, u32[]{:S(2)}) copy-start(bf16[1,2,9,320,320]{4,3,2,1,0:T(8,128)(2,1)} %param.10) | copy-start | bytes 11059204
  26.2 17.3 %copy-start.5 = (s32[4]{0:T(128)S(1)}, s32[4]{0:T(128)}, u32[]{:S(2)}) copy-start(s32[4]{0:T(128)} %refs_0_.3) | copy-start | bytes 52
  37.8 5.6 %collective-permute-start = (bf16[8,120,128]{2,1,0:T(8,128)(2,1)S(1)}, bf16[8,120,128]{2,1,0:T(8,128)(2,1)S(1)}, u32[]{:S(2)}, u32[]{:S(2)}) collective-permute-start(bf16[8,120,128]{2,1,0:T(8,128)(2,1)S(1)} %all_to_all.31.refs_0_), channel_id=1, source_target_pairs={{0,8},{8,16},{16,24},{24,0},{1,9},{9,17},{17,25},{25,1},{2,10},{10... | collective-permute-start | bytes 737288 | tf_op jit(solution)/shard_map/ppermute | solution.py:330
  74.9 5.6 %collective-permute-start.1 = (bf16[8,120,128]{2,1,0:T(8,128)(2,1)S(1)}, bf16[8,120,128]{2,1,0:T(8,128)(2,1)S(1)}, u32[]{:S(2)}, u32[]{:S(2)}) collective-permute-start(bf16[8,120,128]{2,1,0:T(8,128)(2,1)S(1)} %all_to_all.33.refs_0_), channel_id=1, source_target_pairs={{0,8},{8,16},{16,24},{24,0},{1,9},{9,17},{17,25},{25,1},{2,10},{10... | collective-permute-start | bytes 737288 | tf_op jit(solution)/shard_map/ppermute | solution.py:330
